TPU v7x, 128 devices: a whole 4x4x4 slice. The times are simulated.
128 devices in a mesh: lat: 16 (over y, z_lo, core), lon: 8 (over x, z_hi).
Axes of the slice: x: 4, y: 4, z: 4 (z_hi: 2, z_lo: 2; z = z_hi * 2 + z_lo), core: 2. Of those that a mesh axis runs over, the one named last changes fastest.
Arguments:
- tokens: float32 [256, 512, 512], P('lat', 'lon'), may hold values from -20 to 20
- fine_gain: float32 [512], replicated, may hold values from 0.1 to 1.9
- fine_qkv: bfloat16 [512, 1536], replicated
- fine_proj: bfloat16 [512, 512], replicated, may hold values from -0.25 to 0.25
- merge_gain: float32 [2048], replicated, may hold values from 0.1 to 1.9
- merge_weight: bfloat16 [2048, 1024], replicated, may hold values from -0.125 to 0.125
- coarse_gain: float32 [1024], replicated, may hold values from 0.1 to 1.9
- coarse_qkv: bfloat16 [1024, 3072], replicated
- coarse_proj: bfloat16 [1024, 1024], replicated, may hold values from -0.1875 to 0.1875
- expand_weight: bfloat16 [1024, 2048], replicated, may hold values from -0.1875 to 0.1875
- cotangent: float32 [256, 512, 512], P('lat', 'lon'), may hold values from -6 to 6
Outputs:
- result: float32 [256, 512, 512], P('lat', 'lon')
- grad_tokens: float32 [256, 512, 512], P('lat', 'lon')
All inputs are finite; a program needn't handle non-finite values.
Results may differ from a plain program's by a relative error of at most 0.014.
Values may be sent and summed in bfloat16 or wider, within the bound.
A program may use at most 128 MiB of HBM per device.

v0:
```python
import functools
import math

import jax
import jax.numpy as jnp
from jax import lax
from jax.experimental import pallas as pl
from jax.experimental.pallas import tpu as pltpu
from jax.sharding import PartitionSpec as P

F32 = jnp.float32
BF16 = jnp.bfloat16
MESH = pl.DeviceIdType.MESH

ROWS, COLS, CH = 16, 64, 512
CROWS, CCOLS, WIDE = 8, 32, 1024
HEAD = 64
GROUP = 256
TILE = 256
EXP_SCALE = math.log2(math.e) / math.sqrt(HEAD)


def dot(a, b):
    return jnp.dot(a, b, preferred_element_type=F32)


def dot_nt(a, b):
    return lax.dot_general(a, b, (((1,), (1,)), ((), ())), preferred_element_type=F32)


def dot_tn(a, b):
    return lax.dot_general(a, b, (((0,), (0,)), ((), ())), preferred_element_type=F32)


def norm_stats(parts, width):
    mean = sum(jnp.sum(p, axis=-1, keepdims=True) for p in parts) * (1.0 / width)
    centred = [p - mean for p in parts]
    spread = sum(jnp.sum(c * c, axis=-1, keepdims=True) for c in centred) * (1.0 / width)
    return centred, lax.rsqrt(spread + 1e-05)


def norm_grad(parts, grads, gains, width):
    centred, scale = norm_stats(parts, width)
    xhat = [c * scale for c in centred]
    gy = [d * g for d, g in zip(grads, gains)]
    first = sum(jnp.sum(y, axis=-1, keepdims=True) for y in gy) * (1.0 / width)
    second = sum(jnp.sum(y * x, axis=-1, keepdims=True) for y, x in zip(gy, xhat)) * (1.0 / width)
    return [scale * (y - first - x * second) for y, x in zip(gy, xhat)]


def block_diagonal(x, halves):
    zero = jnp.zeros((64, 128), BF16)
    rows = []
    for h in range(4):
        piece = x[:, 128 * (h // 2) : 128 * (h // 2) + 128] * halves[h % 2]
        rows.append(jnp.concatenate([piece, zero] if h < 2 else [zero, piece], axis=1))
    return jnp.concatenate(rows, axis=0)


def per_query(weights, values, low):
    out = []
    for t in range(2):
        lanes = slice(128 * t, 128 * t + 128)
        full = dot_tn(weights[:, lanes], values[:, lanes])
        out.append(jnp.where(low, full[:64], full[64:]))
    return jnp.concatenate(out, axis=1)


def attend(q, k, v, bias, halves, low):
    scores = dot_nt(k, block_diagonal(q, halves)) + bias
    top = jnp.max(scores, axis=0, keepdims=True)
    e = jnp.exp2((scores - top) * EXP_SCALE)
    p = e * (1.0 / jnp.sum(e, axis=0, keepdims=True))
    return p, per_query(p.astype(BF16), v, low)


def attend_grad(q, k, v, p, d_out, halves, low):
    d_diag = block_diagonal(d_out, halves)
    dp = dot_nt(v, d_diag)
    dv = dot(p.astype(BF16), d_diag)
    weighted = p * dp
    ds = ((weighted - p * jnp.sum(weighted, axis=0, keepdims=True)) * (1.0 / math.sqrt(HEAD))).astype(BF16)
    dk = dot(ds, block_diagonal(q, halves))
    dq = per_query(ds, k, low)
    return dq, dk, dv


def aligned(i, step):
    return pl.ds(pl.multiple_of(i * step, step), step)


def kernel(
    tokens, cot, fine_gain, merge_gain, coarse_gain,
    fine_qkv, fine_proj, merge_w, coarse_qkv, coarse_proj, expand_w,
    result, grad,
    tok, cotx, xs, fo, gt, cin, gci, co, xc, gf, res,
    qkv_f, p_f, qkv_c, p_c, n_f, m_f, cells, n_c, m_c, dco, bias,
    w_fq, w_fp, w_m, w_cq, w_cp, w_e,
    load_sem, send_sem, recv_sem,
):
    lat, lon = lax.axis_index("lat"), lax.axis_index("lon")
    n_lat, n_lon = lax.axis_size("lat"), lax.axis_size("lon")
    up, down = lax.rem(lat + n_lat - 1, n_lat), lax.rem(lat + 1, n_lat)
    west, east = lax.rem(lon + n_lon - 1, n_lon), lax.rem(lon + 1, n_lon)

    loads = {}
    for i, (name, src, dst) in enumerate([
        ("tok", tokens, tok.at[0:ROWS, 0:COLS]),
        ("fq", fine_qkv, w_fq),
        ("cot0", cot.at[:, :, 0:128], cotx.at[0:ROWS, 0, 0:COLS]),
        ("cot1", cot.at[:, :, 128:256], cotx.at[0:ROWS, 1, 0:COLS]),
        ("cot2", cot.at[:, :, 256:384], cotx.at[0:ROWS, 2, 0:COLS]),
        ("cot3", cot.at[:, :, 384:512], cotx.at[0:ROWS, 3, 0:COLS]),
        ("e", expand_w, w_e),
        ("fp", fine_proj, w_fp),
        ("m", merge_w, w_m),
        ("cq", coarse_qkv, w_cq),
        ("cp", coarse_proj, w_cp),
    ]):
        loads[name] = pltpu.make_async_copy(src, dst, load_sem.at[i])
        loads[name].start()

    barrier = pltpu.get_barrier_semaphore()
    for a, o in ((up, lon), (lat, west), (up, west), (down, lon), (lat, east), (down, east)):
        pl.semaphore_signal(barrier, inc=1, device_id={"lat": a, "lon": o}, device_id_type=MESH)
    pl.semaphore_wait(barrier, 6)

    def exchange(first, pairs, ahead):
        targets = ((up, lon), (lat, west), (up, west)) if ahead else ((down, lon), (lat, east), (down, east))
        copies = []
        for i, ((src, dst), (a, o)) in enumerate(zip(pairs, targets)):
            copies.append(pltpu.make_async_remote_copy(
                src_ref=src, dst_ref=dst, send_sem=send_sem.at[first + i], recv_sem=recv_sem.at[first + i],
                device_id={"lat": a, "lon": o}, device_id_type=MESH))
            copies[-1].start()
        return copies

    tok_copies = exchange(0, [
        (tokens.at[0:4], tok.at[16:20, 0:64]),
        (tokens.at[:, 0:8], tok.at[0:16, 64:72]),
        (tokens.at[0:4, 0:8], tok.at[16:20, 64:72]),
    ], True)
    for j in range(4):
        loads["cot%d" % j].wait()
    cot_copies = exchange(3, [
        (cotx.at[0:8, :, 0:64], cotx.at[16:24, :, 0:64]),
        (cotx.at[0:16, :, 0:8], cotx.at[0:16, :, 64:72]),
        (cotx.at[0:8, :, 0:8], cotx.at[16:24, :, 64:72]),
    ], True)

    lane = lax.broadcasted_iota(jnp.int32, (1, 128), 1)
    low = lane < 64
    halves = [low.astype(F32).astype(BF16), (lane >= 64).astype(F32).astype(BF16)]
    keys = lax.broadcasted_iota(jnp.int32, (64, GROUP), 0) // 32
    queries = (lax.broadcasted_iota(jnp.int32, (64, GROUP), 1) // 32) % 2
    last = jnp.where(lat == n_lat - 1, 1, 0)
    bias[0] = jnp.zeros((64, GROUP), F32)
    bias[1] = jnp.where((keys != queries) & (last == 1), -jnp.inf, 0.0)

    def product(a, w, tiles, put):
        def step(n, carry):
            put(n, dot(a, w[:, aligned(n, TILE)]))
            return carry
        lax.fori_loop(0, tiles, step, 0)

    def product_t(a, w, tiles, put):
        def step(n, carry):
            put(n, dot_nt(a, w[aligned(n, TILE), :]))
            return carry
        lax.fori_loop(0, tiles, step, 0)

    def store_to(ref, rows):
        def put(n, value):
            ref[rows, aligned(n, TILE)] = value.astype(ref.dtype)
        return put

    def attention(qkv, p_ref, out, first, windows, channels, bias_of):
        groups = channels // GROUP
        def step(w, carry):
            rows = aligned(first + w, 64)
            done = []
            for g in range(groups):
                q, k, v = (qkv[rows, c * channels + g * GROUP : c * channels + (g + 1) * GROUP] for c in range(3))
                done.append(attend(q, k, v, bias[bias_of], halves, low))
            for g, (p, o) in enumerate(done):
                p_ref[rows, g * GROUP : (g + 1) * GROUP] = p
                out[rows, g * GROUP : (g + 1) * GROUP] = o.astype(BF16)
            return carry
        lax.fori_loop(0, windows, step, 0)

    def attention_grad(qkv, p_ref, d_out, first, windows, channels):
        groups = channels // GROUP
        def step(w, carry):
            rows = aligned(first + w, 64)
            done = []
            for g in range(groups):
                lanes = slice(g * GROUP, (g + 1) * GROUP)
                q, k, v = (qkv[rows, c * channels + g * GROUP : c * channels + (g + 1) * GROUP] for c in range(3))
                done.append(attend_grad(q, k, v, p_ref[rows, lanes], d_out[rows, lanes], halves, low))
            for g, grads in enumerate(done):
                for c in range(3):
                    qkv[rows, c * channels + g * GROUP : c * channels + (g + 1) * GROUP] = grads[c].astype(BF16)
            return carry
        lax.fori_loop(0, windows, step, 0)

    def shift_rows(first, count):
        def step(i, carry):
            r = first + i
            xs[r] = tok[r + 4, 4:68, :]
            return carry
        lax.fori_loop(0, count, step, 0)

    def fine_forward(wr):
        def normed(w, carry):
            x = xs[8 * wr : 8 * wr + 8, aligned(w, 8), :].reshape(64, CH)
            (c,), scale = norm_stats([x], CH)
            n_f[aligned(8 * wr + w, 64), :] = (c * scale * fine_gain[...]).astype(BF16)
            return carry
        lax.fori_loop(0, 8, normed, 0)
        half = pl.ds(512 * wr, 512)
        product(n_f[half, :], w_fq, 3 * CH // TILE, store_to(qkv_f, half))
        attention(qkv_f, p_f, m_f, 8 * wr, 8, CH, wr)
        def put(n, value):
            branch = value.astype(BF16).astype(F32)
            lanes = aligned(n, TILE)
            for w in range(8):
                x = xs[8 * wr : 8 * wr + 8, 8 * w : 8 * w + 8, lanes]
                full = x + branch[64 * w : 64 * w + 64].reshape(8, 8, TILE)
                for j in range(2):
                    fo[4 + 8 * wr : 12 + 8 * wr, 2 * n + j, 8 + 8 * w : 16 + 8 * w, :] = full[:, :, 128 * j : 128 * j + 128]
        product(m_f[half, :], w_fp, CH // TILE, put)

    def spread(ref, row, start, count):
        return jnp.concatenate([ref[row, j, pl.ds(start, count, stride=2), :] for j in range(4)], axis=1)

    def merged(i):
        return [spread(fo, 4 + 2 * i + a, 8 + b, 32) for a in range(2) for b in range(2)]

    def merge_forward(wr):
        def normed(i, carry):
            i = 4 * wr + i
            parts, scale = norm_stats(merged(i), 4 * CH)
            for j, c in enumerate(parts):
                gain = merge_gain[:, CH * j : CH * (j + 1)]
                cells[aligned(i, 32), CH * j : CH * (j + 1)] = (c * scale * gain).astype(BF16)
            return carry
        lax.fori_loop(0, 4, normed, 0)
        def put(n, value):
            cin[4 * wr : 4 * wr + 4, 0:32, aligned(n, TILE)] = value.reshape(4, 32, TILE)
        product(cells[128 * wr : 128 * wr + 128, :], w_m, WIDE // TILE, put)

    loads["tok"].wait()
    tok_copies[1].wait_recv()
    shift_rows(0, 12)
    loads["fq"].wait()
    loads["fp"].wait()
    fine_forward(0)
    loads["m"].wait()
    merge_forward(0)
    cin_copies = exchange(6, [(cin.at[0:2, 0:32], cin.at[8:10, 0:32])], True)
    tok_copies[0].wait_recv()
    tok_copies[2].wait_recv()
    shift_rows(12, 4)
    fine_forward(1)
    fo_copies = exchange(9, [
        (fo.at[16:20, :, 8:72], fo.at[0:4, :, 8:72]),
        (fo.at[4:16, :, 64:72], fo.at[4:16, :, 0:8]),
        (fo.at[16:20, :, 64:72], fo.at[0:4, :, 0:8]),
    ], False)
    merge_forward(1)
    cin_copies += [
        pltpu.make_async_remote_copy(
            src_ref=src, dst_ref=dst, send_sem=send_sem.at[7 + i], recv_sem=recv_sem.at[7 + i],
            device_id={"lat": a, "lon": west}, device_id_type=MESH)
        for i, (src, dst, a) in enumerate([
            (cin.at[2:8, 0:8], cin.at[2:8, 32:40], lat),
            (cin.at[0:2, 0:8], cin.at[8:10, 32:40], up),
        ])
    ]
    for c in cin_copies[1:]:
        c.start()

    for c in cot_copies:
        c.wait_recv()
    def gather_cot(i, carry):
        for w in range(4):
            for a in range(2):
                for b in range(2):
                    both = [spread(cotx, 8 + 4 * i + 2 * e + a, 8 + 16 * w + b, 8) for e in range(2)]
                    part = 2 * a + b
                    cells[pl.ds(pl.multiple_of(64 * w + 16 * i, 16), 16), CH * part : CH * (part + 1)] = jnp.concatenate(both, axis=0).astype(BF16)
        return carry
    lax.fori_loop(0, 4, gather_cot, 0)
    loads["e"].wait()
    everything = slice(0, 256)
    product_t(cells[...], w_e, WIDE // TILE, store_to(dco, everything))

    for c in cin_copies:
        c.wait_recv()
    for w in range(4):
        x = cin[2:10, 2 + 8 * w : 10 + 8 * w, :].reshape(64, WIDE)
        xc[64 * w : 64 * w + 64, :] = x
        (c,), scale = norm_stats([x], WIDE)
        n_c[64 * w : 64 * w + 64, :] = (c * scale * coarse_gain[...]).astype(BF16)
    loads["cq"].wait()
    product(n_c[...], w_cq, 3 * WIDE // TILE, store_to(qkv_c, everything))
    attention(qkv_c, p_c, m_c, 0, 4, WIDE, 1)
    loads["cp"].wait()
    def put_co(n, value):
        lanes = aligned(n, TILE)
        full = xc[:, lanes] + value.astype(BF16).astype(F32)
        for w in range(4):
            co[4:12, 8 + 8 * w : 16 + 8 * w, lanes] = full[64 * w : 64 * w + 64].reshape(8, 8, TILE)
    product(m_c[...], w_cp, WIDE // TILE, put_co)
    co_copies = exchange(12, [
        (co.at[8:12, 8:40], co.at[0:4, 8:40]),
        (co.at[4:8, 32:40], co.at[4:8, 0:8]),
        (co.at[8:12, 32:40], co.at[0:4, 0:8]),
    ], False)

    product_t(dco[...], w_cp, WIDE // TILE, store_to(m_c, everything))
    attention_grad(qkv_c, p_c, m_c, 0, 4, WIDE)
    product_t(qkv_c[...], w_cq, WIDE // TILE, store_to(n_c, everything))
    for w in range(4):
        rows = slice(64 * w, 64 * w + 64)
        (d,) = norm_grad([xc[rows, :]], [n_c[rows, :].astype(F32)], [coarse_gain[...]], WIDE)
        gci[2:10, 8 + 8 * w : 16 + 8 * w, :] = (d + dco[rows, :].astype(F32)).reshape(8, 8, WIDE)
    gci_copies = exchange(15, [
        (gci.at[8:10, 8:40], gci.at[0:2, 8:40]),
        (gci.at[2:8, 32:40], gci.at[2:8, 0:8]),
        (gci.at[8:10, 32:40], gci.at[0:2, 0:8]),
    ], False)

    for c in co_copies + fo_copies:
        c.wait_recv()
    for i in range(8):
        n_c[32 * i : 32 * i + 32, :] = co[i, 4:36, :].astype(BF16)
    for a in range(2):
        for b in range(2):
            part = 2 * a + b
            def lift(n, carry):
                w = w_e[:, pl.ds(pl.multiple_of(part * CH + n * TILE, TILE), TILE)]
                lifted = dot(n_c[...], w)
                for s in range(2):
                    j = 2 * n + s
                    for i in range(8):
                        part_fo = fo[2 * i + a, j, pl.ds(4 + b, 32, stride=2), :]
                        res[2 * i + a, j, pl.ds(b, 32, stride=2), :] = part_fo + lifted[32 * i : 32 * i + 32, 128 * s : 128 * s + 128]
                return carry
            lax.fori_loop(0, CH // TILE, lift, 0)
    out_result = [
        pltpu.make_async_copy(res.at[:, j], result.at[:, :, 128 * j : 128 * j + 128], load_sem.at[11 + j])
        for j in range(4)
    ]
    for c in out_result:
        c.start()

    for c in gci_copies:
        c.wait_recv()
    for i in range(8):
        n_c[32 * i : 32 * i + 32, :] = gci[i, 6:38, :].astype(BF16)
    product_t(n_c[...], w_m, 4 * CH // TILE, store_to(cells, everything))
    def merge_grad(i, carry):
        gains = [merge_gain[:, CH * j : CH * (j + 1)] for j in range(4)]
        grads = [cells[aligned(i, 32), CH * j : CH * (j + 1)].astype(F32) for j in range(4)]
        done = norm_grad(merged(i), grads, gains, 4 * CH)
        for a in range(2):
            for b in range(2):
                full = spread(cotx, 4 + 2 * i + a, 4 + b, 32) + done[2 * a + b]
                for j in range(4):
                    gf[2 * i + a, j, pl.ds(b, 32, stride=2), :] = full[:, 128 * j : 128 * j + 128]
        return carry
    lax.fori_loop(0, 8, merge_grad, 0)

    def window(wr, w):
        return jnp.concatenate(
            [gf[8 * wr : 8 * wr + 8, j, aligned(w, 8), :].reshape(64, 128) for j in range(4)], axis=1)
    def to_windows(w, carry):
        for wr in range(2):
            n_f[aligned(8 * wr + w, 64), :] = window(wr, w).astype(BF16)
        return carry
    def fine_grad(wr):
        half = pl.ds(512 * wr, 512)
        product_t(n_f[half, :], w_fp, CH // TILE, store_to(m_f, half))
        attention_grad(qkv_f, p_f, m_f, 8 * wr, 8, CH)
        product_t(qkv_f[half, :], w_fq, CH // TILE, store_to(n_f, half))
        def finish(w, carry):
            cols = aligned(w, 8)
            x = xs[8 * wr : 8 * wr + 8, cols, :].reshape(64, CH)
            dn = n_f[aligned(8 * wr + w, 64), :].astype(F32)
            (d,) = norm_grad([x], [dn], [fine_gain[...]], CH)
            full = (window(wr, w) + d).reshape(8, 8, CH)
            gt[4 + 8 * wr : 12 + 8 * wr, pl.ds(pl.multiple_of(8 + 8 * w, 8), 8), :] = full
            return carry
        lax.fori_loop(0, 8, finish, 0)
    lax.fori_loop(0, 8, to_windows, 0)
    fine_grad(1)
    gt_copies = exchange(18, [(gt.at[16:20, 8:72], gt.at[0:4, 8:72])], False)
    fine_grad(0)
    gt_copies += [
        pltpu.make_async_remote_copy(
            src_ref=src, dst_ref=dst, send_sem=send_sem.at[19 + i], recv_sem=recv_sem.at[19 + i],
            device_id={"lat": a, "lon": east}, device_id_type=MESH)
        for i, (src, dst, a) in enumerate([
            (gt.at[4:16, 64:72], gt.at[4:16, 0:8], lat),
            (gt.at[16:20, 64:72], gt.at[0:4, 0:8], down),
        ])
    ]
    for c in gt_copies[1:]:
        c.start()
    for c in gt_copies:
        c.wait_recv()
    def finish_rows(i, carry):
        xs[i] = gt[i, 4:68, :]
        return carry
    lax.fori_loop(0, ROWS, finish_rows, 0)
    out_grad = pltpu.make_async_copy(xs, grad, load_sem.at[15])
    out_grad.start()
    for c in tok_copies + cot_copies + cin_copies + fo_copies + co_copies + gci_copies + gt_copies:
        c.wait_send()
    for c in out_result + [out_grad]:
        c.wait()


def local(
    tokens, fine_gain, fine_qkv, fine_proj, merge_gain, merge_weight,
    coarse_gain, coarse_qkv, coarse_proj, expand_weight, cotangent,
):
    vmem = pltpu.VMEM
    shape = jax.ShapeDtypeStruct((ROWS, COLS, CH), F32)
    hbm = pl.BlockSpec(memory_space=pl.ANY)
    whole = pl.BlockSpec(memory_space=pltpu.VMEM)
    return pl.pallas_call(
        kernel,
        out_shape=(shape, shape),
        in_specs=[hbm, hbm, whole, whole, whole] + [hbm] * 6,
        out_specs=(hbm, hbm),
        scratch_shapes=[
            vmem((20, 72, CH), F32),
            vmem((24, 4, 72, 128), F32),
            vmem((ROWS, COLS, CH), F32),
            vmem((20, 4, 72, 128), F32),
            vmem((20, 72, CH), F32),
            vmem((10, 40, WIDE), F32),
            vmem((10, 40, WIDE), F32),
            vmem((12, 40, WIDE), F32),
            vmem((256, WIDE), F32),
            vmem((ROWS, 4, COLS, 128), F32),
            vmem((ROWS, 4, COLS, 128), F32),
            vmem((1024, 3 * CH), BF16),
            vmem((1024, CH), F32),
            vmem((256, 3 * WIDE), BF16),
            vmem((256, WIDE), F32),
            vmem((1024, CH), BF16),
            vmem((1024, CH), BF16),
            vmem((256, 4 * CH), BF16),
            vmem((256, WIDE), BF16),
            vmem((256, WIDE), BF16),
            vmem((256, WIDE), BF16),
            vmem((2, 64, GROUP), F32),
            vmem(fine_qkv.shape, BF16),
            vmem(fine_proj.shape, BF16),
            vmem(merge_weight.shape, BF16),
            vmem(coarse_qkv.shape, BF16),
            vmem(coarse_proj.shape, BF16),
            vmem(expand_weight.shape, BF16),
            pltpu.SemaphoreType.DMA((16,)),
            pltpu.SemaphoreType.DMA((21,)),
            pltpu.SemaphoreType.DMA((21,)),
        ],
        compiler_params=pltpu.CompilerParams(
            collective_id=0, has_side_effects=True, vmem_limit_bytes=63 * 1024 * 1024),
    )(
        tokens, cotangent, fine_gain.reshape(1, -1), merge_gain.reshape(1, -1), coarse_gain.reshape(1, -1),
        fine_qkv, fine_proj, merge_weight, coarse_qkv, coarse_proj, expand_weight,
    )


def solution(mesh):
    field = P("lat", "lon", None)
    placed = (field,) + (P(),) * 9 + (field,)
    return jax.shard_map(local, mesh=mesh, in_specs=placed, out_specs=(field, field), check_vma=False)
```

profile of v0, /device:TPU:1, one launch (start us, length us, event | category | flops | bytes accessed | tf_op | source)
XLA Modules:
  0.0 131.2 jit_solution(15197299786264498536)
XLA Ops:
  0.6 125.9 %shard_map.122 = (f32[16,64,512]{2,1,0:T(8,128)}, f32[16,64,512]{2,1,0:T(8,128)}) custom-call(f32[16,64,512]{2,1,0:T(8,128)} %tokens.1, f32[16,64,512]{2,1,0:T(8,128)} %cot.1, f32[1,512]{1,0:T(1,128)} %bitcast.5, f32[1,2048]{1,0:T(1,128)} %bitcast.3, f32[1,1024]{1,0:T(1,128)} %bitcast.4, bf16[512,1536]{1,0:T(8,128)(2,1)} %fine_qkv.1, ...), custom_call_target="tpu_custom_call" | custom-call | tf_op jit(solution)/shard_map/pallas_call | solution.py:433
  126.6 0.0 copy-start
  126.6 3.3 %copy.15 = f32[16,64,512]{2,1,0:T(8,128)} copy(f32[16,64,512]{2,1,0:T(8,128)} %get-tuple-element.4) | data formatting | bytes 4194304
  129.9 0.0 copy-done
  129.9 1.3 %copy.16 = f32[16,64,512]{2,1,0:T(8,128)} copy(f32[16,64,512]{2,1,0:T(8,128)S(1)} %copy-done) | data formatting | bytes 4194304
Async XLA Ops:
  126.6 3.3 %copy-start = (f32[16,64,512]{2,1,0:T(8,128)S(1)}, f32[16,64,512]{2,1,0:T(8,128)}, u32[]{:S(2)}) copy-start(f32[16,64,512]{2,1,0:T(8,128)} %get-tuple-element.5) | copy-start | bytes 6291460
where the time goes:
time: 132 us; the launch traced here: 131 us
  Pallas kernels  126 us (95%)
  local copies, waits for them, and re-layouts  4.61 us (3%)
    pallas_call x1, Pallas kernels, local(): pl.pallas_call(kernel, out_shape=(shape, shape), in_specs=[hbm, hbm, whol...  126 us
    unnamed x4, local copies, waits for them, and re-layouts  4.61 us

commit v1 on v0

--- a/solution.py
+++ b/solution.py
@@ -66,27 +66,35 @@
     return jnp.concatenate(out, axis=1)
 
 
-def attend(q, k, v, bias, halves, low):
-    scores = dot_nt(k, block_diagonal(q, halves)) + bias
-    top = jnp.max(scores, axis=0, keepdims=True)
-    e = jnp.exp2((scores - top) * EXP_SCALE)
-    p = e * (1.0 / jnp.sum(e, axis=0, keepdims=True))
-    return p, per_query(p.astype(BF16), v, low)
-
-
-def attend_grad(q, k, v, p, d_out, halves, low):
-    d_diag = block_diagonal(d_out, halves)
-    dp = dot_nt(v, d_diag)
-    dv = dot(p.astype(BF16), d_diag)
-    weighted = p * dp
-    ds = ((weighted - p * jnp.sum(weighted, axis=0, keepdims=True)) * (1.0 / math.sqrt(HEAD))).astype(BF16)
-    dk = dot(ds, block_diagonal(q, halves))
-    dq = per_query(ds, k, low)
-    return dq, dk, dv
+def attend(items, bias, halves, low):
+    scores = [dot_nt(k, block_diagonal(q, halves)) + bias for q, k, v in items]
+    probs = []
+    for s in scores:
+        e = jnp.exp2((s - jnp.max(s, axis=0, keepdims=True)) * EXP_SCALE)
+        probs.append(e * (1.0 / jnp.sum(e, axis=0, keepdims=True)))
+    return [(p, per_query(p.astype(BF16), v, low)) for p, (q, k, v) in zip(probs, items)]
+
+
+def attend_grad(items, probs, d_outs, halves, low):
+    d_diags = [block_diagonal(d, halves) for d in d_outs]
+    dps = [dot_nt(v, d) for (q, k, v), d in zip(items, d_diags)]
+    dvs = [dot(p.astype(BF16), d) for p, d in zip(probs, d_diags)]
+    dss = []
+    for p, dp in zip(probs, dps):
+        weighted = p * dp
+        dss.append(((weighted - p * jnp.sum(weighted, axis=0, keepdims=True)) * (1.0 / math.sqrt(HEAD))).astype(BF16))
+    dks = [dot(ds, block_diagonal(q, halves)) for ds, (q, k, v) in zip(dss, items)]
+    dqs = [per_query(ds, k, low) for ds, (q, k, v) in zip(dss, items)]
+    return list(zip(dqs, dks, dvs))
 
 
 def aligned(i, step):
-    return pl.ds(pl.multiple_of(i * step, step), step)
+    return pl.ds(i * step, step)
+
+
+def unrolled(first, last, step):
+    for i in range(first, last):
+        step(i, 0)
 
 
 def kernel(
@@ -158,68 +166,62 @@
     bias[1] = jnp.where((keys != queries) & (last == 1), -jnp.inf, 0.0)
 
     def product(a, w, tiles, put):
-        def step(n, carry):
-            put(n, dot(a, w[:, aligned(n, TILE)]))
-            return carry
-        lax.fori_loop(0, tiles, step, 0)
+        for n in range(tiles):
+            put(n, dot(a, w[:, TILE * n : TILE * n + TILE]))
 
     def product_t(a, w, tiles, put):
-        def step(n, carry):
-            put(n, dot_nt(a, w[aligned(n, TILE), :]))
-            return carry
-        lax.fori_loop(0, tiles, step, 0)
+        for n in range(tiles):
+            put(n, dot_nt(a, w[TILE * n : TILE * n + TILE, :]))
 
     def store_to(ref, rows):
         def put(n, value):
-            ref[rows, aligned(n, TILE)] = value.astype(ref.dtype)
+            ref[rows, TILE * n : TILE * n + TILE] = value.astype(ref.dtype)
         return put
 
+    def groups_of(first, windows, channels):
+        for w in range(first, first + windows):
+            for g in range(channels // GROUP):
+                yield pl.ds(64 * w, 64), [pl.ds(c * channels + g * GROUP, GROUP) for c in range(3)]
+
     def attention(qkv, p_ref, out, first, windows, channels, bias_of):
-        groups = channels // GROUP
-        def step(w, carry):
-            rows = aligned(first + w, 64)
-            done = []
-            for g in range(groups):
-                q, k, v = (qkv[rows, c * channels + g * GROUP : c * channels + (g + 1) * GROUP] for c in range(3))
-                done.append(attend(q, k, v, bias[bias_of], halves, low))
-            for g, (p, o) in enumerate(done):
-                p_ref[rows, g * GROUP : (g + 1) * GROUP] = p
-                out[rows, g * GROUP : (g + 1) * GROUP] = o.astype(BF16)
-            return carry
-        lax.fori_loop(0, windows, step, 0)
+        places = list(groups_of(first, windows, channels))
+        items = [tuple(qkv[rows, lanes] for lanes in three) for rows, three in places]
+        done = attend(items, bias[bias_of], halves, low)
+        for (rows, three), (p, o) in zip(places, done):
+            p_ref[rows, three[0]] = p
+            out[rows, three[0]] = o.astype(BF16)
 
     def attention_grad(qkv, p_ref, d_out, first, windows, channels):
-        groups = channels // GROUP
-        def step(w, carry):
-            rows = aligned(first + w, 64)
-            done = []
-            for g in range(groups):
-                lanes = slice(g * GROUP, (g + 1) * GROUP)
-                q, k, v = (qkv[rows, c * channels + g * GROUP : c * channels + (g + 1) * GROUP] for c in range(3))
-                done.append(attend_grad(q, k, v, p_ref[rows, lanes], d_out[rows, lanes], halves, low))
-            for g, grads in enumerate(done):
-                for c in range(3):
-                    qkv[rows, c * channels + g * GROUP : c * channels + (g + 1) * GROUP] = grads[c].astype(BF16)
-            return carry
-        lax.fori_loop(0, windows, step, 0)
+        places = list(groups_of(first, windows, channels))
+        items = [tuple(qkv[rows, lanes] for lanes in three) for rows, three in places]
+        probs = [p_ref[rows, three[0]] for rows, three in places]
+        d_outs = [d_out[rows, three[0]] for rows, three in places]
+        done = attend_grad(items, probs, d_outs, halves, low)
+        for (rows, three), grads in zip(places, done):
+            for lanes, value in zip(three, grads):
+                qkv[rows, lanes] = value.astype(BF16)
 
     def shift_rows(first, count):
         def step(i, carry):
             r = first + i
             xs[r] = tok[r + 4, 4:68, :]
             return carry
-        lax.fori_loop(0, count, step, 0)
-
-    def fine_forward(wr):
+        unrolled(0, count, step)
+
+    def fine_norm(wr):
         def normed(w, carry):
             x = xs[8 * wr : 8 * wr + 8, aligned(w, 8), :].reshape(64, CH)
             (c,), scale = norm_stats([x], CH)
             n_f[aligned(8 * wr + w, 64), :] = (c * scale * fine_gain[...]).astype(BF16)
             return carry
-        lax.fori_loop(0, 8, normed, 0)
+        unrolled(0, 8, normed)
+    def fine_expand(wr):
         half = pl.ds(512 * wr, 512)
         product(n_f[half, :], w_fq, 3 * CH // TILE, store_to(qkv_f, half))
+    def fine_attend(wr):
         attention(qkv_f, p_f, m_f, 8 * wr, 8, CH, wr)
+    def fine_join(wr):
+        half = pl.ds(512 * wr, 512)
         def put(n, value):
             branch = value.astype(BF16).astype(F32)
             lanes = aligned(n, TILE)
@@ -236,7 +238,7 @@
     def merged(i):
         return [spread(fo, 4 + 2 * i + a, 8 + b, 32) for a in range(2) for b in range(2)]
 
-    def merge_forward(wr):
+    def merge_norm(wr):
         def normed(i, carry):
             i = 4 * wr + i
             parts, scale = norm_stats(merged(i), 4 * CH)
@@ -244,7 +246,8 @@
                 gain = merge_gain[:, CH * j : CH * (j + 1)]
                 cells[aligned(i, 32), CH * j : CH * (j + 1)] = (c * scale * gain).astype(BF16)
             return carry
-        lax.fori_loop(0, 4, normed, 0)
+        unrolled(0, 4, normed)
+    def merge_product(wr):
         def put(n, value):
             cin[4 * wr : 4 * wr + 4, 0:32, aligned(n, TILE)] = value.reshape(4, 32, TILE)
         product(cells[128 * wr : 128 * wr + 128, :], w_m, WIDE // TILE, put)
@@ -254,20 +257,28 @@
     shift_rows(0, 12)
     loads["fq"].wait()
     loads["fp"].wait()
-    fine_forward(0)
+    fine_norm(0)
+    fine_expand(0)
+    fine_attend(0)
+    fine_join(0)
     loads["m"].wait()
-    merge_forward(0)
+    merge_norm(0)
+    merge_product(0)
     cin_copies = exchange(6, [(cin.at[0:2, 0:32], cin.at[8:10, 0:32])], True)
     tok_copies[0].wait_recv()
     tok_copies[2].wait_recv()
     shift_rows(12, 4)
-    fine_forward(1)
+    fine_norm(1)
+    fine_expand(1)
+    fine_attend(1)
+    fine_join(1)
     fo_copies = exchange(9, [
         (fo.at[16:20, :, 8:72], fo.at[0:4, :, 8:72]),
         (fo.at[4:16, :, 64:72], fo.at[4:16, :, 0:8]),
         (fo.at[16:20, :, 64:72], fo.at[0:4, :, 0:8]),
     ], False)
-    merge_forward(1)
+    merge_norm(1)
+    merge_product(1)
     cin_copies += [
         pltpu.make_async_remote_copy(
             src_ref=src, dst_ref=dst, send_sem=send_sem.at[7 + i], recv_sem=recv_sem.at[7 + i],
@@ -288,9 +299,9 @@
                 for b in range(2):
                     both = [spread(cotx, 8 + 4 * i + 2 * e + a, 8 + 16 * w + b, 8) for e in range(2)]
                     part = 2 * a + b
-                    cells[pl.ds(pl.multiple_of(64 * w + 16 * i, 16), 16), CH * part : CH * (part + 1)] = jnp.concatenate(both, axis=0).astype(BF16)
+                    cells[pl.ds(64 * w + 16 * i, 16), CH * part : CH * (part + 1)] = jnp.concatenate(both, axis=0).astype(BF16)
         return carry
-    lax.fori_loop(0, 4, gather_cot, 0)
+    unrolled(0, 4, gather_cot)
     loads["e"].wait()
     everything = slice(0, 256)
     product_t(cells[...], w_e, WIDE // TILE, store_to(dco, everything))
@@ -339,7 +350,7 @@
         for b in range(2):
             part = 2 * a + b
             def lift(n, carry):
-                w = w_e[:, pl.ds(pl.multiple_of(part * CH + n * TILE, TILE), TILE)]
+                w = w_e[:, pl.ds(part * CH + n * TILE, TILE)]
                 lifted = dot(n_c[...], w)
                 for s in range(2):
                     j = 2 * n + s
@@ -347,7 +358,7 @@
                         part_fo = fo[2 * i + a, j, pl.ds(4 + b, 32, stride=2), :]
                         res[2 * i + a, j, pl.ds(b, 32, stride=2), :] = part_fo + lifted[32 * i : 32 * i + 32, 128 * s : 128 * s + 128]
                 return carry
-            lax.fori_loop(0, CH // TILE, lift, 0)
+            unrolled(0, CH // TILE, lift)
     out_result = [
         pltpu.make_async_copy(res.at[:, j], result.at[:, :, 128 * j : 128 * j + 128], load_sem.at[11 + j])
         for j in range(4)
@@ -370,7 +381,7 @@
                 for j in range(4):
                     gf[2 * i + a, j, pl.ds(b, 32, stride=2), :] = full[:, 128 * j : 128 * j + 128]
         return carry
-    lax.fori_loop(0, 8, merge_grad, 0)
+    unrolled(0, 8, merge_grad)
 
     def window(wr, w):
         return jnp.concatenate(
@@ -379,24 +390,34 @@
         for wr in range(2):
             n_f[aligned(8 * wr + w, 64), :] = window(wr, w).astype(BF16)
         return carry
-    def fine_grad(wr):
+    def fine_grad_a(wr):
         half = pl.ds(512 * wr, 512)
         product_t(n_f[half, :], w_fp, CH // TILE, store_to(m_f, half))
+    def fine_grad_b(wr):
         attention_grad(qkv_f, p_f, m_f, 8 * wr, 8, CH)
+    def fine_grad_c(wr):
+        half = pl.ds(512 * wr, 512)
         product_t(qkv_f[half, :], w_fq, CH // TILE, store_to(n_f, half))
+    def fine_grad_d(wr):
         def finish(w, carry):
             cols = aligned(w, 8)
             x = xs[8 * wr : 8 * wr + 8, cols, :].reshape(64, CH)
             dn = n_f[aligned(8 * wr + w, 64), :].astype(F32)
             (d,) = norm_grad([x], [dn], [fine_gain[...]], CH)
             full = (window(wr, w) + d).reshape(8, 8, CH)
-            gt[4 + 8 * wr : 12 + 8 * wr, pl.ds(pl.multiple_of(8 + 8 * w, 8), 8), :] = full
+            gt[4 + 8 * wr : 12 + 8 * wr, pl.ds(8 + 8 * w, 8), :] = full
             return carry
-        lax.fori_loop(0, 8, finish, 0)
-    lax.fori_loop(0, 8, to_windows, 0)
-    fine_grad(1)
+        unrolled(0, 8, finish)
+    unrolled(0, 8, to_windows)
+    fine_grad_a(1)
+    fine_grad_b(1)
+    fine_grad_c(1)
+    fine_grad_d(1)
     gt_copies = exchange(18, [(gt.at[16:20, 8:72], gt.at[0:4, 8:72])], False)
-    fine_grad(0)
+    fine_grad_a(0)
+    fine_grad_b(0)
+    fine_grad_c(0)
+    fine_grad_d(0)
     gt_copies += [
         pltpu.make_async_remote_copy(
             src_ref=src, dst_ref=dst, send_sem=send_sem.at[19 + i], recv_sem=recv_sem.at[19 + i],
@@ -413,7 +434,7 @@
     def finish_rows(i, carry):
         xs[i] = gt[i, 4:68, :]
         return carry
-    lax.fori_loop(0, ROWS, finish_rows, 0)
+    unrolled(0, ROWS, finish_rows)
     out_grad = pltpu.make_async_copy(xs, grad, load_sem.at[15])
     out_grad.start()
     for c in tok_copies + cot_copies + cin_copies + fo_copies + co_copies + gci_copies + gt_copies:

time: 132 us -> 120 us (0.909)
  the two profiles are of different devices: /device:TPU:1 before, /device:TPU:8 now
where the time goes in v1:
time: 120 us
  Pallas kernels  115 us (96%)
  local copies, waits for them, and re-layouts  4.61 us (4%)
    pallas_call x1, Pallas kernels, local(): pl.pallas_call(kernel, out_shape=(shape, shape), in_specs=[hbm, hbm, whol...  115 us
    unnamed x4, local copies, waits for them, and re-layouts  4.61 us

profile of v1, /device:TPU:8, one launch (start us, length us, event | category | flops | bytes accessed | tf_op | source)
XLA Modules:
  0.0 119.9 jit_solution(2221834139992334914)
XLA Ops:
  0.6 114.7 %shard_map.122 = (f32[16,64,512]{2,1,0:T(8,128)}, f32[16,64,512]{2,1,0:T(8,128)}) custom-call(f32[16,64,512]{2,1,0:T(8,128)} %tokens.1, f32[16,64,512]{2,1,0:T(8,128)} %cot.1, f32[1,512]{1,0:T(1,128)} %bitcast.5, f32[1,2048]{1,0:T(1,128)} %bitcast.3, f32[1,1024]{1,0:T(1,128)} %bitcast.4, bf16[512,1536]{1,0:T(8,128)(2,1)} %fine_qkv.1, ...), custom_call_target="tpu_custom_call" | custom-call | tf_op jit(solution)/shard_map/pallas_call | solution.py:454
  115.3 0.0 copy-start
  115.3 3.3 %copy.15 = f32[16,64,512]{2,1,0:T(8,128)} copy(f32[16,64,512]{2,1,0:T(8,128)} %get-tuple-element.4) | data formatting | bytes 4194304
  118.6 0.0 copy-done
  118.6 1.3 %copy.16 = f32[16,64,512]{2,1,0:T(8,128)} copy(f32[16,64,512]{2,1,0:T(8,128)S(1)} %copy-done) | data formatting | bytes 4194304
Async XLA Ops:
  115.3 3.3 %copy-start = (f32[16,64,512]{2,1,0:T(8,128)S(1)}, f32[16,64,512]{2,1,0:T(8,128)}, u32[]{:S(2)}) copy-start(f32[16,64,512]{2,1,0:T(8,128)} %get-tuple-element.5) | copy-start | bytes 6291460

commit v2 on v1

v2 whole, which is shorter than its diff:
```python
import functools
import math

import jax
import jax.numpy as jnp
from jax import lax
from jax.experimental import pallas as pl
from jax.experimental.pallas import tpu as pltpu
from jax.sharding import PartitionSpec as P

F32 = jnp.float32
BF16 = jnp.bfloat16
MESH = pl.DeviceIdType.MESH

ROWS, COLS, CH = 16, 64, 512
CROWS, CCOLS, WIDE = 8, 32, 1024
HEAD = 64
GROUP = 256
TILE = 256
EXP_SCALE = math.log2(math.e) / math.sqrt(HEAD)


def dot(a, b):
    return jnp.dot(a, b, preferred_element_type=F32)


def dot_nt(a, b):
    return lax.dot_general(a, b, (((1,), (1,)), ((), ())), preferred_element_type=F32)


def dot_tn(a, b):
    return lax.dot_general(a, b, (((0,), (0,)), ((), ())), preferred_element_type=F32)


def norm_stats(parts, width):
    mean = sum(jnp.sum(p, axis=-1, keepdims=True) for p in parts) * (1.0 / width)
    centred = [p - mean for p in parts]
    spread = sum(jnp.sum(c * c, axis=-1, keepdims=True) for c in centred) * (1.0 / width)
    return centred, lax.rsqrt(spread + 1e-05)


def norm_grad(parts, grads, gains, width):
    centred, scale = norm_stats(parts, width)
    xhat = [c * scale for c in centred]
    gy = [d * g for d, g in zip(grads, gains)]
    first = sum(jnp.sum(y, axis=-1, keepdims=True) for y in gy) * (1.0 / width)
    second = sum(jnp.sum(y * x, axis=-1, keepdims=True) for y, x in zip(gy, xhat)) * (1.0 / width)
    return [scale * (y - first - x * second) for y, x in zip(gy, xhat)]


def block_diagonal(x, halves):
    zero = jnp.zeros((64, 128), BF16)
    rows = []
    for h in range(4):
        piece = x[:, 128 * (h // 2) : 128 * (h // 2) + 128] * halves[h % 2]
        rows.append(jnp.concatenate([piece, zero] if h < 2 else [zero, piece], axis=1))
    return jnp.concatenate(rows, axis=0)


def per_query(weights, values, low):
    out = []
    for t in range(2):
        lanes = slice(128 * t, 128 * t + 128)
        full = dot_tn(weights[:, lanes], values[:, lanes])
        out.append(jnp.where(low, full[:64], full[64:]))
    return jnp.concatenate(out, axis=1)


def attend(items, biases, halves, low):
    scores = [dot_nt(k, block_diagonal(q, halves)) + b for (q, k, v), b in zip(items, biases)]
    probs = []
    for s in scores:
        e = jnp.exp2((s - jnp.max(s, axis=0, keepdims=True)) * EXP_SCALE)
        probs.append(e * (1.0 / jnp.sum(e, axis=0, keepdims=True)))
    return [(p, per_query(p.astype(BF16), v, low)) for p, (q, k, v) in zip(probs, items)]


def attend_grad(items, probs, d_outs, halves, low):
    d_diags = [block_diagonal(d, halves) for d in d_outs]
    dps = [dot_nt(v, d) for (q, k, v), d in zip(items, d_diags)]
    dvs = [dot(p.astype(BF16), d) for p, d in zip(probs, d_diags)]
    dss = []
    for p, dp in zip(probs, dps):
        weighted = p * dp
        dss.append(((weighted - p * jnp.sum(weighted, axis=0, keepdims=True)) * (1.0 / math.sqrt(HEAD))).astype(BF16))
    dks = [dot(ds, block_diagonal(q, halves)) for ds, (q, k, v) in zip(dss, items)]
    dqs = [per_query(ds, k, low) for ds, (q, k, v) in zip(dss, items)]
    return list(zip(dqs, dks, dvs))


def aligned(i, step):
    return pl.ds(i * step, step)


def unrolled(first, last, step):
    for i in range(first, last):
        step(i, 0)


def kernel(
    tokens, cot, fine_gain, merge_gain, coarse_gain,
    fine_qkv, fine_proj, merge_w, coarse_qkv, coarse_proj, expand_w,
    result, grad,
    tok, cotx, xs, fo, cin, gci, co, xc, gf, res,
    qkv_f, p_f, qkv_c, p_c, n_f, m_f, cells, n_c, m_c, dm_c, dco, bias,
    w_fq, w_fp, w_m, w_cq, w_cp, w_e,
    tok_s, tok_d, cot_s, cot_d, cin_s, cin_d, fo_s, fo_d, co_s, co_d, gci_s, gci_d, gt_s, gt_d,
    load_sem, send_sem, recv_sem,
):
    lat, lon = lax.axis_index("lat"), lax.axis_index("lon")
    n_lat, n_lon = lax.axis_size("lat"), lax.axis_size("lon")
    up, down = lax.rem(lat + n_lat - 1, n_lat), lax.rem(lat + 1, n_lat)
    west, east = lax.rem(lon + n_lon - 1, n_lon), lax.rem(lon + 1, n_lon)

    loads = {}
    def load(name, src, dst):
        loads[name] = pltpu.make_async_copy(src, dst, load_sem.at[len(loads)])
        loads[name].start()

    load("tok", tokens, tok.at[0:ROWS, 0:COLS])
    load("fq", fine_qkv, w_fq)
    for j in range(4):
        load("cot%d" % j, cot.at[:, :, 128 * j : 128 * j + 128], cotx.at[0:ROWS, j, 0:COLS])

    barrier = pltpu.get_barrier_semaphore()
    for a, o in ((up, lon), (lat, west), (up, west), (down, lon), (lat, east), (down, east)):
        pl.semaphore_signal(barrier, inc=1, device_id={"lat": a, "lon": o}, device_id_type=MESH)

    def exchange(first, sent, landed, edge, corner, ahead):
        targets = ((up, lon), (lat, west), (up, west)) if ahead else ((down, lon), (lat, east), (down, east))
        sources = (sent[0], sent[1].at[edge[0] : edge[1]], sent[1].at[corner[0] : corner[1]])
        copies = []
        for i, (src, dst, (a, o)) in enumerate(zip(sources, landed, targets)):
            copies.append(pltpu.make_async_remote_copy(
                src_ref=src, dst_ref=dst, send_sem=send_sem.at[first + i], recv_sem=recv_sem.at[first + i],
                device_id={"lat": a, "lon": o}, device_id_type=MESH))
            copies[-1].start()
        return copies

    def pieces(value, start, size):
        return jnp.concatenate([value[8 * a + start : 8 * a + start + size] for a in range(value.shape[0] // 8)], axis=0)

    loads["tok"].wait()
    for i in range(4):
        tok_s[0][i] = tok[i, 0:64, :].astype(BF16)
        tok_s[1][16 * i : 16 * i + 16, :] = jnp.concatenate([tok[4 * i + e, 0:4, :] for e in range(4)], axis=0).astype(BF16)
    pl.semaphore_wait(barrier, 6)
    tok_copies = exchange(0, tok_s, tok_d, (0, 64), (0, 16), True)
    load("fp", fine_proj, w_fp)
    load("m", merge_w, w_m)
    load("e", expand_w, w_e)

    lane = lax.broadcasted_iota(jnp.int32, (1, 128), 1)
    low = lane < 64
    halves = [low.astype(F32).astype(BF16), (lane >= 64).astype(F32).astype(BF16)]
    keys = lax.broadcasted_iota(jnp.int32, (64, GROUP), 0) // 32
    queries = (lax.broadcasted_iota(jnp.int32, (64, GROUP), 1) // 32) % 2
    last = jnp.where(lat == n_lat - 1, 1, 0)
    bias[0] = jnp.zeros((64, GROUP), F32)
    bias[1] = jnp.where((keys != queries) & (last == 1), -jnp.inf, 0.0)

    def product(a, w, tiles, put):
        for n in range(tiles):
            put(n, dot(a, w[:, TILE * n : TILE * n + TILE]))

    def product_t(a, w, tiles, put):
        for n in range(tiles):
            put(n, dot_nt(a, w[TILE * n : TILE * n + TILE, :]))

    def store_to(ref, rows):
        def put(n, value):
            ref[rows, TILE * n : TILE * n + TILE] = value.astype(ref.dtype)
        return put

    def groups_of(first, windows, channels):
        for w in range(first, first + windows):
            for g in range(channels // GROUP):
                yield pl.ds(64 * w, 64), [pl.ds(c * channels + g * GROUP, GROUP) for c in range(3)]

    def attention(qkv, p_ref, out, first, windows, channels, bias_of):
        places = list(groups_of(first, windows, channels))
        items = [tuple(qkv[rows, lanes] for lanes in three) for rows, three in places]
        done = attend(items, [bias[bias_of(rows.start // 64)] for rows, three in places], halves, low)
        for (rows, three), (p, o) in zip(places, done):
            p_ref[rows, three[0]] = p
            out[rows, three[0]] = o.astype(BF16)

    def attention_grad(qkv, p_ref, d_out, first, windows, channels):
        places = list(groups_of(first, windows, channels))
        items = [tuple(qkv[rows, lanes] for lanes in three) for rows, three in places]
        probs = [p_ref[rows, three[0]] for rows, three in places]
        d_outs = [d_out[rows, three[0]] for rows, three in places]
        done = attend_grad(items, probs, d_outs, halves, low)
        for (rows, three), grads in zip(places, done):
            for lanes, value in zip(three, grads):
                qkv[rows, lanes] = value.astype(BF16)

    def window_rows(first, count):
        return slice(64 * first, 64 * (first + count))

    def x_window(w):
        return xs[8 * (w // 8) : 8 * (w // 8) + 8, 8 * (w % 8) : 8 * (w % 8) + 8, :].reshape(64, CH)

    def fine_norm(first, count):
        for w in range(first, first + count):
            (c,), scale = norm_stats([x_window(w)], CH)
            n_f[64 * w : 64 * w + 64, :] = (c * scale * fine_gain[...]).astype(BF16)

    def fine_attend(first, count):
        rows = window_rows(first, count)
        product(n_f[rows, :], w_fq, 3 * CH // TILE, store_to(qkv_f, rows))
        attention(qkv_f, p_f, m_f, first, count, CH, lambda w: w // 8)

    def fine_join(first, count):
        def put(n, value):
            lanes = slice(TILE * n, TILE * n + TILE)
            branch = value.astype(BF16).astype(F32)
            for w in range(first, first + count):
                r, c = 8 * (w // 8), 8 * (w % 8)
                own = branch[64 * (w - first) : 64 * (w - first) + 64]
                full = xs[r : r + 8, c : c + 8, lanes] + own.reshape(8, 8, TILE)
                for j in range(2):
                    fo[4 + r : 12 + r, 2 * n + j, 8 + c : 16 + c, :] = full[:, :, 128 * j : 128 * j + 128]
                if w >= 8:
                    fo_s[0][w - 8, :, lanes] = own[32:].astype(BF16)
                if w % 8 == 7:
                    fo_s[1][32 * (w // 8) : 32 * (w // 8) + 32, lanes] = pieces(own, 4, 4).astype(BF16)
        product(m_f[window_rows(first, count), :], w_fp, CH // TILE, put)

    def spread(ref, row, start, count):
        return jnp.concatenate([ref[row, j, pl.ds(start, count, stride=2), :] for j in range(4)], axis=1)

    def merged(i):
        return [spread(fo, 4 + 2 * i + a, 8 + b, 32) for a in range(2) for b in range(2)]

    for i in range(8):
        xs[i, 0:56, :] = tok[i + 4, 4:60, :]
    fine_norm(0, 7)
    for j in range(4):
        loads["cot%d" % j].wait()
    for i in range(8):
        for j in range(4):
            cot_s[0][i, j] = cotx[i, j, 0:64, :].astype(BF16)
            cot_s[1][i, j] = jnp.concatenate([cotx[2 * i + e, j, 0:8, :] for e in range(2)], axis=0).astype(BF16)
    cot_copies = exchange(3, cot_s, cot_d, (0, 8), (0, 4), True)
    loads["fq"].wait()
    fine_attend(0, 7)
    load("cq", coarse_qkv, w_cq)
    load("cp", coarse_proj, w_cp)
    loads["fp"].wait()
    fine_join(0, 7)
    for c in tok_copies:
        c.wait_recv()
    for i in range(4):
        tok[16 + i, 0:64, :] = tok_d[0][i].astype(F32)
        side = tok_d[1][16 * i : 16 * i + 16, :].astype(F32)
        for e in range(4):
            tok[4 * i + e, 64:68, :] = side[4 * e : 4 * e + 4]
    side = tok_d[2][...].astype(F32)
    for e in range(4):
        tok[16 + e, 64:68, :] = side[4 * e : 4 * e + 4]
    for i in range(8):
        xs[i, 56:64, :] = tok[i + 4, 60:68, :]
        xs[8 + i] = tok[i + 12, 4:68, :]
    fine_norm(7, 9)
    fine_attend(7, 9)
    fine_join(7, 9)
    for i in range(8):
        parts, scale = norm_stats(merged(i), 4 * CH)
        for j, c in enumerate(parts):
            gain = merge_gain[:, CH * j : CH * (j + 1)]
            cells[32 * i : 32 * i + 32, CH * j : CH * (j + 1)] = (c * scale * gain).astype(BF16)
    loads["m"].wait()
    def put_cin(n, value):
        lanes = slice(TILE * n, TILE * n + TILE)
        cin[0:8, 0:32, lanes] = value.reshape(8, 32, TILE)
        cin_s[0][:, :, lanes] = value[0:64].reshape(2, 32, TILE).astype(BF16)
        cin_s[1][:, lanes] = jnp.concatenate([value[32 * i : 32 * i + 2] for i in range(8)], axis=0).astype(BF16)
    product(cells[...], w_m, WIDE // TILE, put_cin)
    cin_copies = exchange(6, cin_s, cin_d, (0, 16), (0, 16), True)
    fo_copies = exchange(9, fo_s, fo_d, (0, 48), (48, 64), False)

    for c in cot_copies:
        c.wait_recv()
    for i in range(8):
        for j in range(4):
            cotx[16 + i, j, 0:64, :] = cot_d[0][i, j].astype(F32)
            side = cot_d[1][i, j].astype(F32)
            for e in range(2):
                cotx[2 * i + e, j, 64:72, :] = side[8 * e : 8 * e + 8]
    for i in range(4):
        for j in range(4):
            side = cot_d[2][i, j].astype(F32)
            for e in range(2):
                cotx[16 + 2 * i + e, j, 64:72, :] = side[8 * e : 8 * e + 8]
    def gather_cot(i, carry):
        for w in range(4):
            for a in range(2):
                for b in range(2):
                    both = [spread(cotx, 8 + 4 * i + 2 * e + a, 8 + 16 * w + b, 8) for e in range(2)]
                    part = 2 * a + b
                    cells[pl.ds(64 * w + 16 * i, 16), CH * part : CH * (part + 1)] = jnp.concatenate(both, axis=0).astype(BF16)
        return carry
    unrolled(0, 4, gather_cot)
    loads["e"].wait()
    everything = slice(0, 256)
    product_t(cells[...], w_e, WIDE // TILE, store_to(dco, everything))

    loads["cp"].wait()
    product_t(dco[...], w_cp, WIDE // TILE, store_to(dm_c, everything))

    for c in cin_copies:
        c.wait_recv()
    for i in range(2):
        cin[8 + i, 0:32, :] = cin_d[0][i].astype(F32)
    side, tip = cin_d[1][...].astype(F32), cin_d[2][...].astype(F32)
    for i in range(2, 8):
        cin[i, 32:34, :] = side[2 * i : 2 * i + 2]
    for i in range(2):
        cin[8 + i, 32:34, :] = tip[2 * i : 2 * i + 2]
    for w in range(4):
        x = cin[2:10, 2 + 8 * w : 10 + 8 * w, :].reshape(64, WIDE)
        xc[64 * w : 64 * w + 64, :] = x
        (c,), scale = norm_stats([x], WIDE)
        n_c[64 * w : 64 * w + 64, :] = (c * scale * coarse_gain[...]).astype(BF16)
    loads["cq"].wait()
    product(n_c[...], w_cq, 3 * WIDE // TILE, store_to(qkv_c, everything))
    attention(qkv_c, p_c, m_c, 0, 4, WIDE, lambda w: 1)
    def put_co(n, value):
        lanes = aligned(n, TILE)
        full = xc[:, lanes] + value.astype(BF16).astype(F32)
        for w in range(4):
            own = full[64 * w : 64 * w + 64]
            co[4:12, 8 + 8 * w : 16 + 8 * w, lanes] = own.reshape(8, 8, TILE)
            co_s[0][w, :, lanes] = own[32:].astype(BF16)
        co_s[1][:, lanes] = pieces(own, 4, 4).astype(BF16)
    product(m_c[...], w_cp, WIDE // TILE, put_co)
    co_copies = exchange(12, co_s, co_d, (0, 16), (16, 32), False)

    attention_grad(qkv_c, p_c, dm_c, 0, 4, WIDE)
    product_t(qkv_c[...], w_cq, WIDE // TILE, store_to(n_c, everything))
    for w in range(4):
        rows = slice(64 * w, 64 * w + 64)
        (d,) = norm_grad([xc[rows, :]], [n_c[rows, :].astype(F32)], [coarse_gain[...]], WIDE)
        full = d + dco[rows, :].astype(F32)
        gci[2:10, 8 + 8 * w : 16 + 8 * w, :] = full.reshape(8, 8, WIDE)
        gci_s[0][w] = full[48:].astype(BF16)
    gci_s[1][...] = pieces(full, 6, 2).astype(BF16)
    gci_copies = exchange(15, gci_s, gci_d, (0, 16), (0, 16), False)

    for c in fo_copies:
        c.wait_recv()
    for w in range(8):
        strip = fo_d[0][w].astype(F32)
        for a in range(4):
            full = tok[a, 4 + 8 * w : 12 + 8 * w, :] + strip[8 * a : 8 * a + 8]
            for j in range(4):
                fo[a, j, 8 + 8 * w : 16 + 8 * w, :] = full[:, 128 * j : 128 * j + 128]
    side, tip = fo_d[1][...].astype(F32), fo_d[2][...].astype(F32)
    for a in range(16):
        full = tok[a, 0:4, :] + (tip[4 * a : 4 * a + 4] if a < 4 else side[4 * a - 16 : 4 * a - 12])
        for j in range(4):
            fo[a, j, 4:8, :] = full[:, 128 * j : 128 * j + 128]
    for c in co_copies:
        c.wait_recv()
    for w in range(4):
        strip = co_d[0][w].astype(F32)
        for a in range(4):
            co[a, 8 + 8 * w : 16 + 8 * w, :] = strip[8 * a : 8 * a + 8]
    side, tip = co_d[1][...].astype(F32), co_d[2][...].astype(F32)
    for a in range(4):
        co[a, 4:8, :] = tip[4 * a : 4 * a + 4]
        co[4 + a, 4:8, :] = side[4 * a : 4 * a + 4]
    for i in range(8):
        n_c[32 * i : 32 * i + 32, :] = co[i, 4:36, :].astype(BF16)
    for a in range(2):
        for b in range(2):
            part = 2 * a + b
            def lift(n, carry):
                w = w_e[:, pl.ds(part * CH + n * TILE, TILE)]
                lifted = dot(n_c[...], w)
                for s in range(2):
                    j = 2 * n + s
                    for i in range(8):
                        part_fo = fo[2 * i + a, j, pl.ds(4 + b, 32, stride=2), :]
                        res[2 * i + a, j, pl.ds(b, 32, stride=2), :] = part_fo + lifted[32 * i : 32 * i + 32, 128 * s : 128 * s + 128]
                return carry
            unrolled(0, CH // TILE, lift)
    out_result = [
        pltpu.make_async_copy(res.at[:, j], result.at[:, :, 128 * j : 128 * j + 128], load_sem.at[12 + j])
        for j in range(4)
    ]
    for c in out_result:
        c.start()

    for c in gci_copies:
        c.wait_recv()
    for w in range(4):
        strip = gci_d[0][w].astype(F32)
        for a in range(2):
            gci[a, 8 + 8 * w : 16 + 8 * w, :] = strip[8 * a : 8 * a + 8]
    side, tip = gci_d[1][...].astype(F32), gci_d[2][...].astype(F32)
    for a in range(6):
        gci[2 + a, 6:8, :] = side[2 * a : 2 * a + 2]
    for a in range(2):
        gci[a, 6:8, :] = tip[12 + 2 * a : 14 + 2 * a]
    for i in range(8):
        n_c[32 * i : 32 * i + 32, :] = gci[i, 6:38, :].astype(BF16)
    product_t(n_c[...], w_m, 4 * CH // TILE, store_to(cells, everything))
    def merge_grad(i, carry):
        gains = [merge_gain[:, CH * j : CH * (j + 1)] for j in range(4)]
        grads = [cells[aligned(i, 32), CH * j : CH * (j + 1)].astype(F32) for j in range(4)]
        done = norm_grad(merged(i), grads, gains, 4 * CH)
        for a in range(2):
            for b in range(2):
                full = spread(cotx, 4 + 2 * i + a, 4 + b, 32) + done[2 * a + b]
                for j in range(4):
                    gf[2 * i + a, j, pl.ds(b, 32, stride=2), :] = full[:, 128 * j : 128 * j + 128]
        return carry
    unrolled(0, 8, merge_grad)

    def window(wr, w):
        return jnp.concatenate(
            [gf[8 * wr : 8 * wr + 8, j, aligned(w, 8), :].reshape(64, 128) for j in range(4)], axis=1)
    gt = tok
    def fine_grad(first, count):
        rows = window_rows(first, count)
        for w in range(first, first + count):
            n_f[64 * w : 64 * w + 64, :] = window(w // 8, w % 8).astype(BF16)
        product_t(n_f[rows, :], w_fp, CH // TILE, store_to(m_f, rows))
        attention_grad(qkv_f, p_f, m_f, first, count, CH)
        product_t(qkv_f[rows, :], w_fq, CH // TILE, store_to(n_f, rows))
        for w in range(first, first + count):
            dn = n_f[64 * w : 64 * w + 64, :].astype(F32)
            (d,) = norm_grad([x_window(w)], [dn], [fine_gain[...]], CH)
            full = window(w // 8, w % 8) + d
            r, c = 8 * (w // 8), 8 * (w % 8)
            gt[4 + r : 12 + r, 8 + c : 16 + c, :] = full.reshape(8, 8, CH)
            if w >= 8:
                gt_s[0][w - 8] = full[32:].astype(BF16)
            if w % 8 == 7:
                gt_s[1][32 * (w // 8) : 32 * (w // 8) + 32, :] = pieces(full, 4, 4).astype(BF16)
    fine_grad(7, 9)
    gt_copies = exchange(18, gt_s, gt_d, (0, 48), (48, 64), False)
    fine_grad(0, 7)
    for c in gt_copies:
        c.wait_recv()
    for w in range(8):
        strip = gt_d[0][w].astype(F32)
        for a in range(4):
            gt[a, 8 + 8 * w : 16 + 8 * w, :] = strip[8 * a : 8 * a + 8]
    side, tip = gt_d[1][...].astype(F32), gt_d[2][...].astype(F32)
    for a in range(16):
        gt[a, 4:8, :] = tip[4 * a : 4 * a + 4] if a < 4 else side[4 * a - 16 : 4 * a - 12]
    for i in range(ROWS):
        xs[i] = gt[i, 4:68, :]
    out_grad = pltpu.make_async_copy(xs, grad, load_sem.at[16])
    out_grad.start()
    for c in tok_copies + cot_copies + cin_copies + fo_copies + co_copies + gci_copies + gt_copies:
        c.wait_send()
    for c in out_result + [out_grad]:
        c.wait()


def exchanged(strip, side, edge, corner):
    vmem = pltpu.VMEM
    return (
        (vmem(strip, BF16), vmem(side, BF16)),
        (vmem(strip, BF16), vmem((edge,) + side[1:], BF16), vmem((corner,) + side[1:], BF16)),
    )


def local(
    tokens, fine_gain, fine_qkv, fine_proj, merge_gain, merge_weight,
    coarse_gain, coarse_qkv, coarse_proj, expand_weight, cotangent,
):
    vmem = pltpu.VMEM
    shape = jax.ShapeDtypeStruct((ROWS, COLS, CH), F32)
    hbm = pl.BlockSpec(memory_space=pl.ANY)
    whole = pl.BlockSpec(memory_space=pltpu.VMEM)
    return pl.pallas_call(
        kernel,
        out_shape=(shape, shape),
        in_specs=[hbm, hbm, whole, whole, whole] + [hbm] * 6,
        out_specs=(hbm, hbm),
        scratch_shapes=[
            vmem((20, 72, CH), F32),
            vmem((24, 4, 72, 128), F32),
            vmem((ROWS, COLS, CH), F32),
            vmem((20, 4, 72, 128), F32),
            vmem((10, 40, WIDE), F32),
            vmem((10, 40, WIDE), F32),
            vmem((12, 40, WIDE), F32),
            vmem((256, WIDE), F32),
            vmem((ROWS, 4, COLS, 128), F32),
            vmem((ROWS, 4, COLS, 128), F32),
            vmem((1024, 3 * CH), BF16),
            vmem((1024, CH), F32),
            vmem((256, 3 * WIDE), BF16),
            vmem((256, WIDE), F32),
            vmem((1024, CH), BF16),
            vmem((1024, CH), BF16),
            vmem((256, 4 * CH), BF16),
            vmem((256, WIDE), BF16),
            vmem((256, WIDE), BF16),
            vmem((256, WIDE), BF16),
            vmem((256, WIDE), BF16),
            vmem((2, 64, GROUP), F32),
            vmem(fine_qkv.shape, BF16),
            vmem(fine_proj.shape, BF16),
            vmem(merge_weight.shape, BF16),
            vmem(coarse_qkv.shape, BF16),
            vmem(coarse_proj.shape, BF16),
            vmem(expand_weight.shape, BF16),
            *exchanged((4, 64, CH), (64, CH), 64, 16),
            *exchanged((8, 4, 64, 128), (8, 4, 16, 128), 8, 4),
            *exchanged((2, 32, WIDE), (16, WIDE), 16, 16),
            *exchanged((8, 32, CH), (64, CH), 48, 16),
            *exchanged((4, 32, WIDE), (32, WIDE), 16, 16),
            *exchanged((4, 16, WIDE), (16, WIDE), 16, 16),
            *exchanged((8, 32, CH), (64, CH), 48, 16),
            pltpu.SemaphoreType.DMA((17,)),
            pltpu.SemaphoreType.DMA((21,)),
            pltpu.SemaphoreType.DMA((21,)),
        ],
        compiler_params=pltpu.CompilerParams(
            collective_id=0, has_side_effects=True, vmem_limit_bytes=63 * 1024 * 1024),
    )(
        tokens, cotangent, fine_gain.reshape(1, -1), merge_gain.reshape(1, -1), coarse_gain.reshape(1, -1),
        fine_qkv, fine_proj, merge_weight, coarse_qkv, coarse_proj, expand_weight,
    )


def solution(mesh):
    field = P("lat", "lon", None)
    placed = (field,) + (P(),) * 9 + (field,)
    return jax.shard_map(local, mesh=mesh, in_specs=placed, out_specs=(field, field), check_vma=False)
```

time: 120 us -> 62.4 us (0.52)
  the two profiles are of different devices: /device:TPU:8 before, /device:TPU:1 now
where the time goes in v2:
time: 62.4 us; the launch traced here: 62.2 us
  Pallas kernels  57 us (91%)
  local copies, waits for them, and re-layouts  4.61 us (7%)
  between operations  0.65 us (1%)
    pallas_call x1, Pallas kernels, local(): pl.pallas_call(kernel, out_shape=(shape, shape), in_specs=[hbm, hbm, whol...  57 us
    unnamed x4, local copies, waits for them, and re-layouts  4.61 us

profile of v2, /device:TPU:1, one launch (start us, length us, event | category | flops | bytes accessed | tf_op | source)
XLA Modules:
  0.0 62.2 jit_solution(5109057629217092552)
XLA Ops:
  0.6 57.0 %shard_map.122 = (f32[16,64,512]{2,1,0:T(8,128)}, f32[16,64,512]{2,1,0:T(8,128)}) custom-call(f32[16,64,512]{2,1,0:T(8,128)} %tokens.1, f32[16,64,512]{2,1,0:T(8,128)} %cot.1, f32[1,512]{1,0:T(1,128)} %bitcast.5, f32[1,2048]{1,0:T(1,128)} %bitcast.3, f32[1,1024]{1,0:T(1,128)} %bitcast.4, bf16[512,1536]{1,0:T(8,128)(2,1)} %fine_qkv.1, ...), custom_call_target="tpu_custom_call" | custom-call | tf_op jit(solution)/shard_map/pallas_call | solution.py:481
  57.6 0.0 copy-start
  57.6 3.3 %copy.15 = f32[16,64,512]{2,1,0:T(8,128)} copy(f32[16,64,512]{2,1,0:T(8,128)} %get-tuple-element.4) | data formatting | bytes 4194304
  60.9 0.0 copy-done
  60.9 1.3 %copy.16 = f32[16,64,512]{2,1,0:T(8,128)} copy(f32[16,64,512]{2,1,0:T(8,128)S(1)} %copy-done) | data formatting | bytes 4194304
Async XLA Ops:
  57.6 3.3 %copy-start = (f32[16,64,512]{2,1,0:T(8,128)S(1)}, f32[16,64,512]{2,1,0:T(8,128)}, u32[]{:S(2)}) copy-start(f32[16,64,512]{2,1,0:T(8,128)} %get-tuple-element.5) | copy-start | bytes 6291460

commit v3 on v2

--- a/solution.py
+++ b/solution.py
@@ -104,7 +104,7 @@
     tok, cotx, xs, fo, cin, gci, co, xc, gf, res,
     qkv_f, p_f, qkv_c, p_c, n_f, m_f, cells, n_c, m_c, dm_c, dco, bias,
     w_fq, w_fp, w_m, w_cq, w_cp, w_e,
-    tok_s, tok_d, cot_s, cot_d, cin_s, cin_d, fo_s, fo_d, co_s, co_d, gci_s, gci_d, gt_s, gt_d,
+    tok_s, tok_d, cot_s, cot_d, dco_s, dco_d, cin_s, cin_d, fo_s, fo_d, co_s, co_d, gci_s, gci_d, gt_s, gt_d,
     load_sem, send_sem, recv_sem,
 ):
     lat, lon = lax.axis_index("lat"), lax.axis_index("lon")
@@ -112,19 +112,21 @@
     up, down = lax.rem(lat + n_lat - 1, n_lat), lax.rem(lat + 1, n_lat)
     west, east = lax.rem(lon + n_lon - 1, n_lon), lax.rem(lon + 1, n_lon)
 
+    barrier = pltpu.get_barrier_semaphore()
+    for a, o in ((up, lon), (lat, west), (up, west), (down, lon), (lat, east), (down, east)):
+        pl.semaphore_signal(barrier, inc=1, device_id={"lat": a, "lon": o}, device_id_type=MESH)
+
     loads = {}
     def load(name, src, dst):
         loads[name] = pltpu.make_async_copy(src, dst, load_sem.at[len(loads)])
         loads[name].start()
 
-    load("tok", tokens, tok.at[0:ROWS, 0:COLS])
+    load("top", tokens.at[0:4], tok.at[0:4, 0:COLS])
+    load("side", tokens.at[4:ROWS, 0:8], tok.at[4:ROWS, 0:8])
+    load("tok", tokens.at[4:ROWS, 8:COLS], tok.at[4:ROWS, 8:COLS])
     load("fq", fine_qkv, w_fq)
     for j in range(4):
         load("cot%d" % j, cot.at[:, :, 128 * j : 128 * j + 128], cotx.at[0:ROWS, j, 0:COLS])
-
-    barrier = pltpu.get_barrier_semaphore()
-    for a, o in ((up, lon), (lat, west), (up, west), (down, lon), (lat, east), (down, east)):
-        pl.semaphore_signal(barrier, inc=1, device_id={"lat": a, "lon": o}, device_id_type=MESH)
 
     def exchange(first, sent, landed, edge, corner, ahead):
         targets = ((up, lon), (lat, west), (up, west)) if ahead else ((down, lon), (lat, east), (down, east))
@@ -140,15 +142,17 @@
     def pieces(value, start, size):
         return jnp.concatenate([value[8 * a + start : 8 * a + start + size] for a in range(value.shape[0] // 8)], axis=0)
 
-    loads["tok"].wait()
+    loads["top"].wait()
+    loads["side"].wait()
     for i in range(4):
         tok_s[0][i] = tok[i, 0:64, :].astype(BF16)
         tok_s[1][16 * i : 16 * i + 16, :] = jnp.concatenate([tok[4 * i + e, 0:4, :] for e in range(4)], axis=0).astype(BF16)
     pl.semaphore_wait(barrier, 6)
-    tok_copies = exchange(0, tok_s, tok_d, (0, 64), (0, 16), True)
+    tok_copies = exchange(0, tok_s, tok_d, (16, 64), (0, 16), True)
+    loads["tok"].wait()
     load("fp", fine_proj, w_fp)
+    load("e", expand_w, w_e)
     load("m", merge_w, w_m)
-    load("e", expand_w, w_e)
 
     lane = lax.broadcasted_iota(jnp.int32, (1, 128), 1)
     low = lane < 64
@@ -230,30 +234,48 @@
     def spread(ref, row, start, count):
         return jnp.concatenate([ref[row, j, pl.ds(start, count, stride=2), :] for j in range(4)], axis=1)
 
-    def merged(i):
-        return [spread(fo, 4 + 2 * i + a, 8 + b, 32) for a in range(2) for b in range(2)]
+    def merged(row, col, count):
+        return [spread(fo, 4 + 2 * row + a, 8 + 2 * col + b, count) for a in range(2) for b in range(2)]
+
+    batch_a = [(i, 0, 32, 32 * i) for i in range(4)] + [(4 + i, 0, 16, 128 + 16 * i) for i in range(4)]
+    batch_b = [(4 + i, 16, 16, 192 + 16 * i) for i in range(4)]
 
     for i in range(8):
         xs[i, 0:56, :] = tok[i + 4, 4:60, :]
     fine_norm(0, 7)
     for j in range(4):
         loads["cot%d" % j].wait()
-    for i in range(8):
+    for i in range(4):
         for j in range(4):
             cot_s[0][i, j] = cotx[i, j, 0:64, :].astype(BF16)
-            cot_s[1][i, j] = jnp.concatenate([cotx[2 * i + e, j, 0:8, :] for e in range(2)], axis=0).astype(BF16)
-    cot_copies = exchange(3, cot_s, cot_d, (0, 8), (0, 4), True)
+            cot_s[1][i, j] = jnp.concatenate([cotx[4 * i + e, j, 0:4, :] for e in range(4)], axis=0).astype(BF16)
+    cot_copies = exchange(3, cot_s, cot_d, (1, 4), (0, 1), True)
     loads["fq"].wait()
     fine_attend(0, 7)
     load("cq", coarse_qkv, w_cq)
     load("cp", coarse_proj, w_cp)
     loads["fp"].wait()
     fine_join(0, 7)
+    for i in range(8):
+        for a in range(2):
+            for b in range(2):
+                part = 2 * a + b
+                cells[32 * i : 32 * i + 32, CH * part : CH * (part + 1)] = spread(cotx, 2 * i + a, b, 32).astype(BF16)
+    loads["e"].wait()
+    everything = slice(0, 256)
+    def put_dco(n, value):
+        lanes = slice(TILE * n, TILE * n + TILE)
+        dco_s[0][:, :, lanes] = value[0:128].reshape(4, 32, TILE).astype(BF16)
+        dco_s[1][:, lanes] = jnp.concatenate([value[32 * i : 32 * i + 4] for i in range(8)], axis=0).astype(BF16)
+        co[0:4, 0:32, lanes] = value[128:256].reshape(4, 32, TILE)
+    product_t(cells[...], w_e, WIDE // TILE, put_dco)
+    dco_copies = exchange(21, dco_s, dco_d, (16, 32), (0, 16), True)
     for c in tok_copies:
         c.wait_recv()
     for i in range(4):
         tok[16 + i, 0:64, :] = tok_d[0][i].astype(F32)
-        side = tok_d[1][16 * i : 16 * i + 16, :].astype(F32)
+    for i in range(1, 4):
+        side = tok_d[1][16 * i - 16 : 16 * i, :].astype(F32)
         for e in range(4):
             tok[4 * i + e, 64:68, :] = side[4 * e : 4 * e + 4]
     side = tok_d[2][...].astype(F32)
@@ -262,55 +284,50 @@
     for i in range(8):
         xs[i, 56:64, :] = tok[i + 4, 60:68, :]
         xs[8 + i] = tok[i + 12, 4:68, :]
-    fine_norm(7, 9)
-    fine_attend(7, 9)
-    fine_join(7, 9)
-    for i in range(8):
-        parts, scale = norm_stats(merged(i), 4 * CH)
-        for j, c in enumerate(parts):
-            gain = merge_gain[:, CH * j : CH * (j + 1)]
-            cells[32 * i : 32 * i + 32, CH * j : CH * (j + 1)] = (c * scale * gain).astype(BF16)
+    fine_norm(7, 5)
+    fine_attend(7, 5)
+    fine_join(7, 5)
+    def merge_norm(batch):
+        for row, col, count, at in batch:
+            parts, scale = norm_stats(merged(row, col, count), 4 * CH)
+            for j, c in enumerate(parts):
+                gain = merge_gain[:, CH * j : CH * (j + 1)]
+                cells[at : at + count, CH * j : CH * (j + 1)] = (c * scale * gain).astype(BF16)
+    merge_norm(batch_a)
     loads["m"].wait()
     def put_cin(n, value):
         lanes = slice(TILE * n, TILE * n + TILE)
-        cin[0:8, 0:32, lanes] = value.reshape(8, 32, TILE)
+        cin[0:4, 0:32, lanes] = value[0:128].reshape(4, 32, TILE)
+        cin[4:8, 0:16, lanes] = value[128:192].reshape(4, 16, TILE)
         cin_s[0][:, :, lanes] = value[0:64].reshape(2, 32, TILE).astype(BF16)
-        cin_s[1][:, lanes] = jnp.concatenate([value[32 * i : 32 * i + 2] for i in range(8)], axis=0).astype(BF16)
-    product(cells[...], w_m, WIDE // TILE, put_cin)
+        starts = [32 * i for i in range(4)] + [128 + 16 * i for i in range(4)]
+        cin_s[1][:, lanes] = jnp.concatenate([value[i : i + 2] for i in starts], axis=0).astype(BF16)
+    product(cells[0:192, :], w_m, WIDE // TILE, put_cin)
     cin_copies = exchange(6, cin_s, cin_d, (0, 16), (0, 16), True)
-    fo_copies = exchange(9, fo_s, fo_d, (0, 48), (48, 64), False)
-
-    for c in cot_copies:
-        c.wait_recv()
-    for i in range(8):
-        for j in range(4):
-            cotx[16 + i, j, 0:64, :] = cot_d[0][i, j].astype(F32)
-            side = cot_d[1][i, j].astype(F32)
-            for e in range(2):
-                cotx[2 * i + e, j, 64:72, :] = side[8 * e : 8 * e + 8]
+    fine_norm(12, 4)
+    fine_attend(12, 4)
+    fine_join(12, 4)
+    merge_norm(batch_b)
+    def put_cin_b(n, value):
+        cin[4:8, 16:32, TILE * n : TILE * n + TILE] = value.reshape(4, 16, TILE)
+    product(cells[192:256, :], w_m, WIDE // TILE, put_cin_b)
+
+    for c in dco_copies:
+        c.wait_recv()
     for i in range(4):
-        for j in range(4):
-            side = cot_d[2][i, j].astype(F32)
-            for e in range(2):
-                cotx[16 + 2 * i + e, j, 64:72, :] = side[8 * e : 8 * e + 8]
-    def gather_cot(i, carry):
-        for w in range(4):
-            for a in range(2):
-                for b in range(2):
-                    both = [spread(cotx, 8 + 4 * i + 2 * e + a, 8 + 16 * w + b, 8) for e in range(2)]
-                    part = 2 * a + b
-                    cells[pl.ds(64 * w + 16 * i, 16), CH * part : CH * (part + 1)] = jnp.concatenate(both, axis=0).astype(BF16)
-        return carry
-    unrolled(0, 4, gather_cot)
-    loads["e"].wait()
-    everything = slice(0, 256)
-    product_t(cells[...], w_e, WIDE // TILE, store_to(dco, everything))
-
+        co[4 + i, 0:32, :] = dco_d[0][i].astype(F32)
+    side, tip = dco_d[1][...].astype(F32), dco_d[2][...].astype(F32)
+    for i in range(4):
+        co[i, 32:36, :] = side[4 * i : 4 * i + 4]
+        co[4 + i, 32:36, :] = tip[4 * i : 4 * i + 4]
+    for w in range(4):
+        dco[64 * w : 64 * w + 64, :] = co[0:8, 4 + 8 * w : 12 + 8 * w, :].reshape(64, WIDE).astype(BF16)
     loads["cp"].wait()
     product_t(dco[...], w_cp, WIDE // TILE, store_to(dm_c, everything))
 
     for c in cin_copies:
         c.wait_recv()
+    fo_copies = exchange(9, fo_s, fo_d, (0, 48), (48, 64), False)
     for i in range(2):
         cin[8 + i, 0:32, :] = cin_d[0][i].astype(F32)
     side, tip = cin_d[1][...].astype(F32), cin_d[2][...].astype(F32)
@@ -348,6 +365,58 @@
     gci_s[1][...] = pieces(full, 6, 2).astype(BF16)
     gci_copies = exchange(15, gci_s, gci_d, (0, 16), (0, 16), False)
 
+    def merge_grad(batch):
+        first, last = batch[0][3], batch[-1][3] + batch[-1][2]
+        for row, col, count, at in batch:
+            n_c[at : at + count, :] = gci[row, 6 + col : 6 + col + count, :].astype(BF16)
+        product_t(n_c[first:last, :], w_m, 4 * CH // TILE, store_to(cells, slice(first, last)))
+        gains = [merge_gain[:, CH * j : CH * (j + 1)] for j in range(4)]
+        for row, col, count, at in batch:
+            grads = [cells[at : at + count, CH * j : CH * (j + 1)].astype(F32) for j in range(4)]
+            done = norm_grad(merged(row, col, count), grads, gains, 4 * CH)
+            for a in range(2):
+                for b in range(2):
+                    full = spread(cotx, 4 + 2 * row + a, 4 + 2 * col + b, count) + done[2 * a + b]
+                    for j in range(4):
+                        gf[2 * row + a, j, pl.ds(2 * col + b, count, stride=2), :] = full[:, 128 * j : 128 * j + 128]
+
+    def window(wr, w):
+        return jnp.concatenate(
+            [gf[8 * wr : 8 * wr + 8, j, aligned(w, 8), :].reshape(64, 128) for j in range(4)], axis=1)
+    gt = tok
+    def fine_grad(first, count):
+        rows = window_rows(first, count)
+        for w in range(first, first + count):
+            n_f[64 * w : 64 * w + 64, :] = window(w // 8, w % 8).astype(BF16)
+        product_t(n_f[rows, :], w_fp, CH // TILE, store_to(m_f, rows))
+        attention_grad(qkv_f, p_f, m_f, first, count, CH)
+        product_t(qkv_f[rows, :], w_fq, CH // TILE, store_to(n_f, rows))
+        for w in range(first, first + count):
+            dn = n_f[64 * w : 64 * w + 64, :].astype(F32)
+            (d,) = norm_grad([x_window(w)], [dn], [fine_gain[...]], CH)
+            full = window(w // 8, w % 8) + d
+            r, c = 8 * (w // 8), 8 * (w % 8)
+            gt[4 + r : 12 + r, 8 + c : 16 + c, :] = full.reshape(8, 8, CH)
+            if w >= 8:
+                gt_s[0][w - 8] = full[32:].astype(BF16)
+            if w % 8 == 7:
+                gt_s[1][32 * (w // 8) : 32 * (w // 8) + 32, :] = pieces(full, 4, 4).astype(BF16)
+    for c in cot_copies:
+        c.wait_recv()
+    for i in range(4):
+        for j in range(4):
+            cotx[16 + i, j, 0:64, :] = cot_d[0][i, j].astype(F32)
+    for i in range(1, 5):
+        for j in range(4):
+            side = (cot_d[1][i - 1, j] if i < 4 else cot_d[2][0, j]).astype(F32)
+            for e in range(4):
+                cotx[4 * i + e, j, 64:68, :] = side[4 * e : 4 * e + 4]
+    merge_grad(batch_b)
+    fine_grad(12, 4)
+    gt_first = pltpu.make_async_remote_copy(
+        src_ref=gt_s[0].at[4:8], dst_ref=gt_d[0].at[4:8], send_sem=send_sem.at[24], recv_sem=recv_sem.at[24],
+        device_id={"lat": down, "lon": lon}, device_id_type=MESH)
+    gt_first.start()
     for c in fo_copies:
         c.wait_recv()
     for w in range(8):
@@ -387,7 +456,7 @@
                 return carry
             unrolled(0, CH // TILE, lift)
     out_result = [
-        pltpu.make_async_copy(res.at[:, j], result.at[:, :, 128 * j : 128 * j + 128], load_sem.at[12 + j])
+        pltpu.make_async_copy(res.at[:, j], result.at[:, :, 128 * j : 128 * j + 128], load_sem.at[14 + j])
         for j in range(4)
     ]
     for c in out_result:
@@ -404,45 +473,12 @@
         gci[2 + a, 6:8, :] = side[2 * a : 2 * a + 2]
     for a in range(2):
         gci[a, 6:8, :] = tip[12 + 2 * a : 14 + 2 * a]
-    for i in range(8):
-        n_c[32 * i : 32 * i + 32, :] = gci[i, 6:38, :].astype(BF16)
-    product_t(n_c[...], w_m, 4 * CH // TILE, store_to(cells, everything))
-    def merge_grad(i, carry):
-        gains = [merge_gain[:, CH * j : CH * (j + 1)] for j in range(4)]
-        grads = [cells[aligned(i, 32), CH * j : CH * (j + 1)].astype(F32) for j in range(4)]
-        done = norm_grad(merged(i), grads, gains, 4 * CH)
-        for a in range(2):
-            for b in range(2):
-                full = spread(cotx, 4 + 2 * i + a, 4 + b, 32) + done[2 * a + b]
-                for j in range(4):
-                    gf[2 * i + a, j, pl.ds(b, 32, stride=2), :] = full[:, 128 * j : 128 * j + 128]
-        return carry
-    unrolled(0, 8, merge_grad)
-
-    def window(wr, w):
-        return jnp.concatenate(
-            [gf[8 * wr : 8 * wr + 8, j, aligned(w, 8), :].reshape(64, 128) for j in range(4)], axis=1)
-    gt = tok
-    def fine_grad(first, count):
-        rows = window_rows(first, count)
-        for w in range(first, first + count):
-            n_f[64 * w : 64 * w + 64, :] = window(w // 8, w % 8).astype(BF16)
-        product_t(n_f[rows, :], w_fp, CH // TILE, store_to(m_f, rows))
-        attention_grad(qkv_f, p_f, m_f, first, count, CH)
-        product_t(qkv_f[rows, :], w_fq, CH // TILE, store_to(n_f, rows))
-        for w in range(first, first + count):
-            dn = n_f[64 * w : 64 * w + 64, :].astype(F32)
-            (d,) = norm_grad([x_window(w)], [dn], [fine_gain[...]], CH)
-            full = window(w // 8, w % 8) + d
-            r, c = 8 * (w // 8), 8 * (w % 8)
-            gt[4 + r : 12 + r, 8 + c : 16 + c, :] = full.reshape(8, 8, CH)
-            if w >= 8:
-                gt_s[0][w - 8] = full[32:].astype(BF16)
-            if w % 8 == 7:
-                gt_s[1][32 * (w // 8) : 32 * (w // 8) + 32, :] = pieces(full, 4, 4).astype(BF16)
-    fine_grad(7, 9)
-    gt_copies = exchange(18, gt_s, gt_d, (0, 48), (48, 64), False)
+    merge_grad(batch_a)
+    fine_grad(7, 5)
+    gt_copies = exchange(
+        18, (gt_s[0].at[0:4], gt_s[1]), (gt_d[0].at[0:4], gt_d[1], gt_d[2]), (0, 48), (48, 64), False)
     fine_grad(0, 7)
+    gt_copies.append(gt_first)
     for c in gt_copies:
         c.wait_recv()
     for w in range(8):
@@ -454,9 +490,9 @@
         gt[a, 4:8, :] = tip[4 * a : 4 * a + 4] if a < 4 else side[4 * a - 16 : 4 * a - 12]
     for i in range(ROWS):
         xs[i] = gt[i, 4:68, :]
-    out_grad = pltpu.make_async_copy(xs, grad, load_sem.at[16])
+    out_grad = pltpu.make_async_copy(xs, grad, load_sem.at[13])
     out_grad.start()
-    for c in tok_copies + cot_copies + cin_copies + fo_copies + co_copies + gci_copies + gt_copies:
+    for c in tok_copies + cot_copies + dco_copies + cin_copies + fo_copies + co_copies + gci_copies + gt_copies:
         c.wait_send()
     for c in out_result + [out_grad]:
         c.wait()
@@ -478,14 +514,14 @@
     shape = jax.ShapeDtypeStruct((ROWS, COLS, CH), F32)
     hbm = pl.BlockSpec(memory_space=pl.ANY)
     whole = pl.BlockSpec(memory_space=pltpu.VMEM)
-    return pl.pallas_call(
+    done = pl.pallas_call(
         kernel,
         out_shape=(shape, shape),
         in_specs=[hbm, hbm, whole, whole, whole] + [hbm] * 6,
         out_specs=(hbm, hbm),
         scratch_shapes=[
             vmem((20, 72, CH), F32),
-            vmem((24, 4, 72, 128), F32),
+            vmem((20, 4, 72, 128), F32),
             vmem((ROWS, COLS, CH), F32),
             vmem((20, 4, 72, 128), F32),
             vmem((10, 40, WIDE), F32),
@@ -512,16 +548,17 @@
             vmem(coarse_qkv.shape, BF16),
             vmem(coarse_proj.shape, BF16),
             vmem(expand_weight.shape, BF16),
-            *exchanged((4, 64, CH), (64, CH), 64, 16),
-            *exchanged((8, 4, 64, 128), (8, 4, 16, 128), 8, 4),
+            *exchanged((4, 64, CH), (64, CH), 48, 16),
+            *exchanged((4, 4, 64, 128), (4, 4, 16, 128), 3, 1),
+            *exchanged((4, 32, WIDE), (32, WIDE), 16, 16),
             *exchanged((2, 32, WIDE), (16, WIDE), 16, 16),
             *exchanged((8, 32, CH), (64, CH), 48, 16),
             *exchanged((4, 32, WIDE), (32, WIDE), 16, 16),
             *exchanged((4, 16, WIDE), (16, WIDE), 16, 16),
             *exchanged((8, 32, CH), (64, CH), 48, 16),
-            pltpu.SemaphoreType.DMA((17,)),
-            pltpu.SemaphoreType.DMA((21,)),
-            pltpu.SemaphoreType.DMA((21,)),
+            pltpu.SemaphoreType.DMA((18,)),
+            pltpu.SemaphoreType.DMA((25,)),
+            pltpu.SemaphoreType.DMA((25,)),
         ],
         compiler_params=pltpu.CompilerParams(
             collective_id=0, has_side_effects=True, vmem_limit_bytes=63 * 1024 * 1024),
@@ -529,6 +566,29 @@
         tokens, cotangent, fine_gain.reshape(1, -1), merge_gain.reshape(1, -1), coarse_gain.reshape(1, -1),
         fine_qkv, fine_proj, merge_weight, coarse_qkv, coarse_proj, expand_weight,
     )
+    return pl.pallas_call(
+        hand_over,
+        out_shape=(shape, shape),
+        in_specs=[hbm, hbm],
+        out_specs=(hbm, hbm),
+        scratch_shapes=[
+            pltpu.VMEM((8, 4, COLS, CH), F32), pltpu.SemaphoreType.DMA((8,)), pltpu.SemaphoreType.DMA((8,))],
+    )(*done)
+
+
+def hand_over(result, grad, result_out, grad_out, held, load_sem, store_sem):
+    loads, stores = [], []
+    for i, (src, dst) in enumerate(((result, result_out), (grad, grad_out))):
+        for part in range(4):
+            rows, slot = pl.ds(4 * part, 4), 4 * i + part
+            loads.append(pltpu.make_async_copy(src.at[rows], held.at[slot], load_sem.at[slot]))
+            stores.append(pltpu.make_async_copy(held.at[slot], dst.at[rows], store_sem.at[slot]))
+            loads[-1].start()
+    for load, store in zip(loads, stores):
+        load.wait()
+        store.start()
+    for store in stores:
+        store.wait()
 
 
 def solution(mesh):

time: 62.4 us -> 58.8 us (0.942)
  local copies, waits for them, and re-layouts: 4.61 us -> 0 us
  Pallas kernels: 57 us -> 57.8 us
    unnamed x4 -> x0, local copies, waits for them, and re-layouts: 4.61 us -> none
    pallas_call x0 -> x1, Pallas kernels: none -> 3.58 us  [local(): pl.pallas_call(hand_over, out_shape=(shape, shape), in_specs=[hbm, hbm],...]
    pallas_call x1, Pallas kernels: 57 us -> 54.2 us  [local(): pl.pallas_call(kernel, out_shape=(shape, shape), in_specs=[hbm, hbm, whol...]
where the time goes in v3:
time: 58.8 us; the launch traced here: 58.6 us
  Pallas kernels  57.8 us (98%)
  between operations  0.8 us (1%)
    pallas_call x1, Pallas kernels, local(): pl.pallas_call(kernel, out_shape=(shape, shape), in_specs=[hbm, hbm, whol...  54.2 us
    pallas_call x1, Pallas kernels, local(): pl.pallas_call(hand_over, out_shape=(shape, shape), in_specs=[hbm, hbm],...  3.58 us

profile of v3, /device:TPU:1, one launch (start us, length us, event | category | flops | bytes accessed | tf_op | source)
XLA Modules:
  0.0 58.6 jit_solution(1668319438172976951)
XLA Ops:
  0.6 54.2 %shard_map.122 = (f32[16,64,512]{2,1,0:T(8,128)}, f32[16,64,512]{2,1,0:T(8,128)}) custom-call(f32[16,64,512]{2,1,0:T(8,128)} %tokens.1, f32[16,64,512]{2,1,0:T(8,128)} %cot.1, f32[1,512]{1,0:T(1,128)} %bitcast.5, f32[1,2048]{1,0:T(1,128)} %bitcast.3, f32[1,1024]{1,0:T(1,128)} %bitcast.4, bf16[512,1536]{1,0:T(8,128)(2,1)} %fine_qkv.1, ...), custom_call_target="tpu_custom_call" | custom-call | tf_op jit(solution)/shard_map/pallas_call | solution.py:517
  54.9 3.6 %shard_map.123 = (f32[16,64,512]{2,1,0:T(8,128)}, f32[16,64,512]{2,1,0:T(8,128)}) custom-call(f32[16,64,512]{2,1,0:T(8,128)} %get-tuple-element.4.result, f32[16,64,512]{2,1,0:T(8,128)} %get-tuple-element.5.grad), custom_call_target="tpu_custom_call" | custom-call | tf_op jit(solution)/shard_map/pallas_call | solution.py:569

commit v4 on v3

--- a/solution.py
+++ b/solution.py
@@ -136,7 +136,8 @@
             copies.append(pltpu.make_async_remote_copy(
                 src_ref=src, dst_ref=dst, send_sem=send_sem.at[first + i], recv_sem=recv_sem.at[first + i],
                 device_id={"lat": a, "lon": o}, device_id_type=MESH))
-            copies[-1].start()
+        for copy in reversed(copies):
+            copy.start()
         return copies
 
     def pieces(value, start, size):
@@ -325,21 +326,25 @@
     loads["cp"].wait()
     product_t(dco[...], w_cp, WIDE // TILE, store_to(dm_c, everything))
 
-    for c in cin_copies:
-        c.wait_recv()
-    fo_copies = exchange(9, fo_s, fo_d, (0, 48), (48, 64), False)
+    cin_copies[0].wait_recv()
     for i in range(2):
         cin[8 + i, 0:32, :] = cin_d[0][i].astype(F32)
+    def coarse_norm(w):
+        x = cin[2:10, 2 + 8 * w : 10 + 8 * w, :].reshape(64, WIDE)
+        xc[64 * w : 64 * w + 64, :] = x
+        (c,), scale = norm_stats([x], WIDE)
+        n_c[64 * w : 64 * w + 64, :] = (c * scale * coarse_gain[...]).astype(BF16)
+    for w in range(3):
+        coarse_norm(w)
+    for c in cin_copies[1:]:
+        c.wait_recv()
+    fo_copies = exchange(9, fo_s, fo_d, (0, 48), (48, 64), False)
     side, tip = cin_d[1][...].astype(F32), cin_d[2][...].astype(F32)
     for i in range(2, 8):
         cin[i, 32:34, :] = side[2 * i : 2 * i + 2]
     for i in range(2):
         cin[8 + i, 32:34, :] = tip[2 * i : 2 * i + 2]
-    for w in range(4):
-        x = cin[2:10, 2 + 8 * w : 10 + 8 * w, :].reshape(64, WIDE)
-        xc[64 * w : 64 * w + 64, :] = x
-        (c,), scale = norm_stats([x], WIDE)
-        n_c[64 * w : 64 * w + 64, :] = (c * scale * coarse_gain[...]).astype(BF16)
+    coarse_norm(3)
     loads["cq"].wait()
     product(n_c[...], w_cq, 3 * WIDE // TILE, store_to(qkv_c, everything))
     attention(qkv_c, p_c, m_c, 0, 4, WIDE, lambda w: 1)
@@ -478,23 +483,33 @@
     gt_copies = exchange(
         18, (gt_s[0].at[0:4], gt_s[1]), (gt_d[0].at[0:4], gt_d[1], gt_d[2]), (0, 48), (48, 64), False)
     fine_grad(0, 7)
+    for i in range(4, ROWS):
+        xs[i, 8:64, :] = gt[i, 12:68, :]
+    out_grad = [
+        pltpu.make_async_copy(xs.at[rows, cols], grad.at[rows, cols], load_sem.at[slot])
+        for rows, cols, slot in (
+            (pl.ds(4, 12), pl.ds(8, 56), 13), (pl.ds(4, 12), pl.ds(0, 8), 18), (pl.ds(0, 4), pl.ds(0, 64), 19))
+    ]
+    out_grad[0].start()
     gt_copies.append(gt_first)
     for c in gt_copies:
         c.wait_recv()
+    side, tip = gt_d[1][...].astype(F32), gt_d[2][...].astype(F32)
+    for a in range(16):
+        gt[a, 4:8, :] = tip[4 * a : 4 * a + 4] if a < 4 else side[4 * a - 16 : 4 * a - 12]
+    for i in range(4, ROWS):
+        xs[i, 0:8, :] = gt[i, 4:12, :]
+    out_grad[1].start()
     for w in range(8):
         strip = gt_d[0][w].astype(F32)
         for a in range(4):
             gt[a, 8 + 8 * w : 16 + 8 * w, :] = strip[8 * a : 8 * a + 8]
-    side, tip = gt_d[1][...].astype(F32), gt_d[2][...].astype(F32)
-    for a in range(16):
-        gt[a, 4:8, :] = tip[4 * a : 4 * a + 4] if a < 4 else side[4 * a - 16 : 4 * a - 12]
-    for i in range(ROWS):
+    for i in range(4):
         xs[i] = gt[i, 4:68, :]
-    out_grad = pltpu.make_async_copy(xs, grad, load_sem.at[13])
-    out_grad.start()
+    out_grad[2].start()
     for c in tok_copies + cot_copies + dco_copies + cin_copies + fo_copies + co_copies + gci_copies + gt_copies:
         c.wait_send()
-    for c in out_result + [out_grad]:
+    for c in out_result + out_grad:
         c.wait()
 
 
@@ -556,7 +571,7 @@
             *exchanged((4, 32, WIDE), (32, WIDE), 16, 16),
             *exchanged((4, 16, WIDE), (16, WIDE), 16, 16),
             *exchanged((8, 32, CH), (64, CH), 48, 16),
-            pltpu.SemaphoreType.DMA((18,)),
+            pltpu.SemaphoreType.DMA((20,)),
             pltpu.SemaphoreType.DMA((25,)),
             pltpu.SemaphoreType.DMA((25,)),
         ],

time: 58.8 us -> 55.7 us (0.947)
  Pallas kernels: 57.8 us -> 54.8 us
    pallas_call x1, Pallas kernels: 54.2 us -> 51.2 us  [local(): pl.pallas_call(kernel, out_shape=(shape, shape), in_specs=[hbm, hbm, whol...]
where the time goes in v4:
time: 55.7 us; the launch traced here: 55.6 us
  Pallas kernels  54.8 us (98%)
  between operations  0.8 us (1%)
    pallas_call x1, Pallas kernels, local(): pl.pallas_call(kernel, out_shape=(shape, shape), in_specs=[hbm, hbm, whol...  51.2 us
    pallas_call x1, Pallas kernels, local(): pl.pallas_call(hand_over, out_shape=(shape, shape), in_specs=[hbm, hbm],...  3.58 us

profile of v4, /device:TPU:1, one launch (start us, length us, event | category | flops | bytes accessed | tf_op | source)
XLA Modules:
  0.0 55.6 jit_solution(1752016114216674752)
XLA Ops:
  0.6 51.2 %shard_map.122 = (f32[16,64,512]{2,1,0:T(8,128)}, f32[16,64,512]{2,1,0:T(8,128)}) custom-call(f32[16,64,512]{2,1,0:T(8,128)} %tokens.1, f32[16,64,512]{2,1,0:T(8,128)} %cot.1, f32[1,512]{1,0:T(1,128)} %bitcast.5, f32[1,2048]{1,0:T(1,128)} %bitcast.3, f32[1,1024]{1,0:T(1,128)} %bitcast.4, bf16[512,1536]{1,0:T(8,128)(2,1)} %fine_qkv.1, ...), custom_call_target="tpu_custom_call" | custom-call | tf_op jit(solution)/shard_map/pallas_call | solution.py:532
  51.8 3.6 %shard_map.123 = (f32[16,64,512]{2,1,0:T(8,128)}, f32[16,64,512]{2,1,0:T(8,128)}) custom-call(f32[16,64,512]{2,1,0:T(8,128)} %get-tuple-element.4.result, f32[16,64,512]{2,1,0:T(8,128)} %get-tuple-element.5.grad), custom_call_target="tpu_custom_call" | custom-call | tf_op jit(solution)/shard_map/pallas_call | solution.py:584

commit v5 on v4

--- a/solution.py
+++ b/solution.py
@@ -244,6 +244,8 @@
     for i in range(8):
         xs[i, 0:56, :] = tok[i + 4, 4:60, :]
     fine_norm(0, 7)
+    loads["fq"].wait()
+    fine_attend(0, 7)
     for j in range(4):
         loads["cot%d" % j].wait()
     for i in range(4):
@@ -251,8 +253,6 @@
             cot_s[0][i, j] = cotx[i, j, 0:64, :].astype(BF16)
             cot_s[1][i, j] = jnp.concatenate([cotx[4 * i + e, j, 0:4, :] for e in range(4)], axis=0).astype(BF16)
     cot_copies = exchange(3, cot_s, cot_d, (1, 4), (0, 1), True)
-    loads["fq"].wait()
-    fine_attend(0, 7)
     load("cq", coarse_qkv, w_cq)
     load("cp", coarse_proj, w_cp)
     loads["fp"].wait()

time: 55.7 us -> 56.8 us (1.020)
  Pallas kernels: 54.8 us -> 55.8 us
    pallas_call x1, Pallas kernels: 51.2 us -> 52.2 us  [local(): pl.pallas_call(kernel, out_shape=(shape, shape), in_specs=[hbm, hbm, whol...]
where the time goes in v5:
time: 56.8 us; the launch traced here: 56.6 us
  Pallas kernels  55.8 us (98%)
  between operations  0.8 us (1%)
    pallas_call x1, Pallas kernels, local(): pl.pallas_call(kernel, out_shape=(shape, shape), in_specs=[hbm, hbm, whol...  52.2 us
    pallas_call x1, Pallas kernels, local(): pl.pallas_call(hand_over, out_shape=(shape, shape), in_specs=[hbm, hbm],...  3.58 us

profile of v5, /device:TPU:1, one launch (start us, length us, event | category | flops | bytes accessed | tf_op | source)
XLA Modules:
  0.0 56.6 jit_solution(6948175444870175667)
XLA Ops:
  0.6 52.2 %shard_map.122 = (f32[16,64,512]{2,1,0:T(8,128)}, f32[16,64,512]{2,1,0:T(8,128)}) custom-call(f32[16,64,512]{2,1,0:T(8,128)} %tokens.1, f32[16,64,512]{2,1,0:T(8,128)} %cot.1, f32[1,512]{1,0:T(1,128)} %bitcast.5, f32[1,2048]{1,0:T(1,128)} %bitcast.3, f32[1,1024]{1,0:T(1,128)} %bitcast.4, bf16[512,1536]{1,0:T(8,128)(2,1)} %fine_qkv.1, ...), custom_call_target="tpu_custom_call" | custom-call | tf_op jit(solution)/shard_map/pallas_call | solution.py:532
  52.9 3.6 %shard_map.123 = (f32[16,64,512]{2,1,0:T(8,128)}, f32[16,64,512]{2,1,0:T(8,128)}) custom-call(f32[16,64,512]{2,1,0:T(8,128)} %get-tuple-element.4.result, f32[16,64,512]{2,1,0:T(8,128)} %get-tuple-element.5.grad), custom_call_target="tpu_custom_call" | custom-call | tf_op jit(solution)/shard_map/pallas_call | solution.py:584
